TPU v7x, 256 devices: a whole 4x4x8 slice. The times are simulated.
256 devices in a mesh: node: 64 (over y_hi, z, x), feat: 4 (over y_lo, core).
Axes of the slice: x: 4, y: 4 (y_hi: 2, y_lo: 2; y = y_hi * 2 + y_lo), z: 8, core: 2. Of those that a mesh axis runs over, the one named last changes fastest.
Arguments:
- features: bfloat16 [65536, 256], P('node', 'feat'), may hold values from -6 to 6
- w_self: bfloat16 [256, 256], P('feat'), may hold values from -0.375 to 0.375
- w_neigh: bfloat16 [256, 256], P('feat'), may hold values from -0.375 to 0.375
- tile_rows: int32 [16384], P('node'), may hold values from 0 to 7
- tile_cols: int32 [16384], P('node'), may hold values from 0 to 511
- tile_count: int32 [64], P('node'), may hold values from 64 to 256, as said below
- edge_bits: int32 [16384, 16, 128], P('node'), may hold values from 0 to 255
- cotangent: float32 [65536, 256], P('node', 'feat'), may hold values from -6 to 6
Outputs:
- activated: float32 [65536, 256], P('node', 'feat')
- grad_features: float32 [65536, 256], P('node', 'feat')
- grad_self: float32 [256, 256], P('feat')
- grad_neigh: float32 [256, 256], P('feat')
Inputs may be any that keep to these rules, and one draw needn't show every extreme that they name: `tile_count`: slots of a block at or beyond its count are ignored; some block is full in every draw.
All inputs are finite; a program needn't handle non-finite values.
Results may differ from a plain program's by a relative error of at most 0.0028.
Values may be sent and summed in bfloat16 or wider, within the bound.
A program may use at most 128 MiB of HBM per device.

v0:
```python
import jax
import jax.numpy as jnp
from jax import lax
from jax.sharding import PartitionSpec as P


def unpack_bits(words):
    shifts = jnp.arange(8, dtype=jnp.int32)
    planes = jnp.bitwise_and(jnp.right_shift(words[:, :, None, :], shifts[None, None, :, None]), 1)
    return planes.reshape(words.shape[0], words.shape[1] * 8, words.shape[2])


def local(features, w_self, w_neigh, tile_rows, tile_cols, tile_count, edge_bits, cotangent):
    hi = lax.Precision.HIGHEST
    tile_size = edge_bits.shape[2]
    per_block = tile_rows.shape[0]
    block_rows = features.shape[0]
    feat_cols = features.shape[1]
    row_tiles = block_rows // tile_size
    live_tiles = (jnp.arange(per_block, dtype=jnp.int32) < tile_count[0]).astype(jnp.float32)
    mask_f32 = unpack_bits(edge_bits).astype(jnp.float32) * live_tiles[:, None, None]
    mask_bf16 = mask_f32.astype(jnp.bfloat16)
    rowhot = (tile_rows[:, None] == jnp.arange(row_tiles, dtype=jnp.int32)[None, :]).astype(
        jnp.float32
    )
    counts = jnp.einsum("tr,tp->rp", rowhot, jnp.sum(mask_f32, axis=1), precision=hi).reshape(
        block_rows
    )
    degree = jnp.maximum(counts, 1.0)
    gathered = lax.all_gather(features, "node", axis=0, tiled=True)
    all_tiles = gathered.shape[0] // tile_size
    picked = jnp.take(gathered.reshape(all_tiles, tile_size, feat_cols), tile_cols, axis=0)
    products = jnp.einsum("tqp,tqf->tpf", mask_bf16, picked, preferred_element_type=jnp.float32)
    summed = jnp.einsum("tr,tpf->rpf", rowhot, products, precision=hi).reshape(
        block_rows, feat_cols
    )
    averaged = (summed / degree[:, None]).astype(jnp.bfloat16)
    partial_z = jnp.dot(features, w_self, preferred_element_type=jnp.float32) + jnp.dot(
        averaged, w_neigh, preferred_element_type=jnp.float32
    )
    pre_own = lax.psum_scatter(partial_z, "feat", scatter_dimension=1, tiled=True)
    sigmoid_z = jax.nn.sigmoid(pre_own)
    activated = pre_own * sigmoid_z
    grad_own = cotangent * sigmoid_z * (1.0 + pre_own * (1.0 - sigmoid_z))
    grad_full = lax.all_gather(grad_own, "feat", axis=1, tiled=True)
    scaled = jnp.dot(grad_full, w_neigh.astype(jnp.float32).T, precision=hi) / degree[:, None]
    source = jnp.take(scaled.reshape(row_tiles, tile_size, feat_cols), tile_rows, axis=0)
    contrib = jnp.einsum("tqp,tpf->tqf", mask_f32, source, precision=hi)
    accum = jnp.zeros((all_tiles, tile_size, feat_cols), jnp.float32).at[tile_cols].add(contrib)
    returned = lax.psum_scatter(
        accum.reshape(all_tiles * tile_size, feat_cols), "node", scatter_dimension=0, tiled=True
    )
    direct = jnp.dot(grad_full, w_self.astype(jnp.float32).T, precision=hi)
    part_self = jnp.dot(features.astype(jnp.float32).T, grad_full, precision=hi)
    part_neigh = jnp.dot(averaged.astype(jnp.float32).T, grad_full, precision=hi)
    grad_self, grad_neigh = lax.psum((part_self, part_neigh), "node")
    grad_features = direct + returned
    return (activated, grad_features, grad_self, grad_neigh)


def solution(mesh):
    placed = (
        P("node", "feat"),
        P("feat", None),
        P("feat", None),
        P("node"),
        P("node"),
        P("node"),
        P("node", None, None),
        P("node", "feat"),
    )
    return jax.shard_map(
        local,
        mesh=mesh,
        in_specs=placed,
        out_specs=(P("node", "feat"), P("node", "feat"), P("feat", None), P("feat", None)),
        check_vma=False,
    )
```

profile of v0, /device:TPU:24, one launch (start us, length us, event | category | flops | bytes accessed | tf_op | source)
XLA Modules:
  0.0 1358.7 jit_solution(8074949666454659282)
XLA Ops:
  7.2 0.7 all-gather.3.cloned.1.call-update
  8.6 0.1 shift_right_arithmetic.28
  8.7 0.7 compare_select_fusion.1
  9.4 0.7 compare_and_fusion.1
  10.1 4.4 multiply_reduce_fusion
  14.5 0.8 fusion.25
  15.4 1.2 fusion.39
  16.6 143.6 %all-gather.3.cloned.1.call-done = bf16[65536,64]{0,1:T(8,128)(2,1)} async-done(((bf16[1024,64]{0,1:T(8,128)(2,1)}), bf16[65536,64]{0,1:T(8,128)(2,1)}) %all-gather.3.cloned.1.call-update) | async-done | bytes 8388624 | tf_op jit(solution)/shard_map/all_gather | solution.py:30
  160.2 9.0 copy_bitcast_fusion.1
  169.2 6.6 gather_fusion
  175.8 6.0 fusion.6
  181.8 7.5 fusion.8
  189.3 1.3 convolution_add_fusion
  190.7 0.0 all-gather.5.cloned.1.call-start
  190.7 20.4 %reduce-scatter.3.cloned.1.call-done = f32[1024,64]{0,1:T(8,128)} async-done(((f32[1024,256]{0,1:T(8,128)}), f32[1024,64]{0,1:T(8,128)}) %reduce-scatter.3.cloned.1.call-update) | async-done | bytes 262160 | tf_op jit(solution)/shard_map/reduce_scatter | solution.py:41
  211.1 1.9 add_multiply_fusion
  213.1 25.2 %all-gather.5.cloned.1.call-done = f32[1024,256]{0,1:T(8,128)} async-done(((f32[1024,64]{0,1:T(8,128)}), f32[1024,256]{0,1:T(8,128)}) %all-gather.5.cloned.1.call-update) | async-done | bytes 1048592 | tf_op jit(solution)/shard_map/all_gather | solution.py:45
  238.3 1.7 fusion.24
  240.1 4.4 gather_fusion.1
  244.5 37.2 %fusion.3 = f32[256,128,64]{1,2,0:T(8,128)} fusion(f32[256,128,64]{1,2,0:T(8,128)} %gather_fusion.1, f32[256]{0:T(256)S(1)} %get-tuple-element.9, s32[128]{0:T(128)S(1)} %shift_right_arithmetic.28, s32[256,16,128]{2,1,0:T(8,128)S(1)} %copy-done.3, pred[256]{0:T(512)(128)(4,1)S(1)} %compare_and_fusion), kind=kOutput, calls=%fused_computation.8 | convolution fusion | flops 3240099840 | bytes 18876160 | tf_op jit(solution)/shard_map/tqp,tpf->tqf/dot_general | solution.py:48
  281.7 7.9 broadcast_in_dim.38
  289.5 39.4 %scatter_fusion = f32[512,128,64]{1,2,0:T(8,128)} fusion(f32[512,128,64]{1,2,0:T(8,128)} %broadcast_in_dim.38, s32[256]{0:T(256)S(1)} %compare_select_fusion.1, f32[256,128,64]{1,2,0:T(8,128)} %fusion.3), kind=kCustom, calls=%fused_computation.2 | custom fusion | flops 2097152 | bytes 25166848 | tf_op jit(solution)/shard_map/scatter-add | solution.py:49
  328.9 11.4 copy_bitcast_fusion
  340.3 0.0 all-reduce.3.cloned.1.call-start
  340.4 1.1 copy-done.2
  341.5 1.3 convolution_bitcast_fusion
  342.8 1.3 fusion.36
  344.2 397.3 %reduce-scatter.5.cloned.1.call-done = f32[1024,64]{0,1:T(8,128)} async-done(((f32[65536,64]{0,1:T(8,128)}), f32[1024,64]{0,1:T(8,128)}) %reduce-scatter.5.cloned.1.call-update) | async-done | bytes 262160 | tf_op jit(solution)/shard_map/reduce_scatter | solution.py:50
  741.4 2.2 convolution_add_fusion.1
  743.6 605.6 %all-reduce.3.cloned.1.call-done = (f32[64,256]{1,0:T(8,128)}, f32[64,256]{1,0:T(8,128)}) async-done(((f32[64,256]{1,0:T(8,128)}, f32[64,256]{1,0:T(8,128)}), (f32[64,256]{1,0:T(8,128)}, f32[64,256]{1,0:T(8,128)})) %all-reduce.3.cloned.1.call-update) | async-done | bytes 131088 | tf_op jit(solution)/shard_map/psum | solution.py:56
  1349.2 1.5 copy.36
  1350.7 1.5 copy.37
  (26 shorter events, 0.3 us)
Async XLA Ops:
  7.2 182.2 %copy-start = (bf16[64,256]{1,0:T(8,128)(2,1)S(1)}, bf16[64,256]{1,0:T(8,128)(2,1)}, u32[]{:S(2)}) copy-start(bf16[64,256]{1,0:T(8,128)(2,1)} %param.10) | copy-start | bytes 98308
  7.2 153.0 %all-gather.3.cloned.1.call-start = ((), (), s32[]{:S(2)}) async-start(), calls=%async_computation.2 | async-start | bytes 8519680 | tf_op jit(solution)/shard_map/all_gather | solution.py:30
  7.9 203.2 %reduce-scatter.3.cloned.1.call-start = ((), (), s32[]{:S(2)}) async-start(), calls=%async_computation.3 | async-start | bytes 1310720 | tf_op jit(solution)/shard_map/reduce_scatter | solution.py:41
  169.2 6.6 copy-start.3
  175.8 6.0 copy-start.6
  190.7 47.7 %all-gather.5.cloned.1.call-start = ((), (), s32[]{:S(2)}) async-start(), calls=%async_computation.4 | async-start | bytes 1310720 | tf_op jit(solution)/shard_map/all_gather | solution.py:45
  213.0 528.4 %reduce-scatter.5.cloned.1.call-start = ((), (), s32[]{:S(2)}) async-start(), calls=%async_computation.5 | async-start | bytes 17039360 | tf_op jit(solution)/shard_map/reduce_scatter | solution.py:50
  340.3 1011.9 %copy-start.1 = (bf16[64,256]{1,0:T(8,128)(2,1)S(1)}, bf16[64,256]{1,0:T(8,128)(2,1)}, u32[]{:S(2)}) copy-start(bf16[64,256]{1,0:T(8,128)(2,1)} %param.10) | copy-start | bytes 98308
  340.3 1.2 copy-start.2
  340.3 1.2 copy-start.4
  340.3 401.1 %copy-start.5 = (bf16[64,256]{1,0:T(8,128)(2,1)S(1)}, bf16[64,256]{1,0:T(8,128)(2,1)}, u32[]{:S(2)}) copy-start(bf16[64,256]{1,0:T(8,128)(2,1)} %param.9) | copy-start | bytes 98308
  340.3 1008.9 %all-reduce.3.cloned.1.call-start = ((), (), s32[]{:S(2)}) async-start(), calls=%async_computation.6 | async-start | bytes 262144 | tf_op jit(solution)/shard_map/psum | solution.py:56
Sparse Core Ops, SparseCore 0:
  11.5 148.6 all-gather.2
  190.8 20.2 reduce-scatter.2
  213.6 24.6 all-gather.4
  340.5 400.9 reduce-scatter.4
  744.7 604.4 all-reduce.2
where the time goes:
time: 1360 us
  waiting for transfers between devices  1190 us (88%)
  matrix products  60.6 us (4%)
  other arithmetic  47.2 us (3%)
  local copies, waits for them, and re-layouts  43.5 us (3%)
  between operations  14.5 us (1%)
    psum x1, waiting for transfers between devices, local(): grad_self, grad_neigh = lax.psum((part_self, part_neigh), 'node')  606 us
    reduce_scatter x1, waiting for transfers between devices, local(): lax.psum_scatter(accum.reshape(all_tiles * tile_size, feat_cols), 'node',...  397 us
    all_gather x1, waiting for transfers between devices, local(): gathered = lax.all_gather(features, 'node', axis=0, tiled=True)  144 us
    scatter-add x1, other arithmetic, local(): jnp.zeros((all_tiles, tile_size, feat_cols), jnp.float32).at[tile_cols]  39.4 us
    dot_general x1, matrix products, local(): contrib = jnp.einsum('tqp,tpf->tqf', mask_f32, source, precision=hi)  37.2 us
  transfers between devices with their start and end apart: 5, of which 5 were waited for; matrix products, arithmetic and copies ran while one was open for 1% of the time, Pallas kernels for 0%

commit v1 on v0

v1 whole, which is shorter than its diff:
```python
import jax
import jax.numpy as jnp
from jax import lax
from jax.experimental import pallas as pl
from jax.experimental.pallas import tpu as pltpu
from jax.sharding import PartitionSpec as P

MESH = pl.DeviceIdType.MESH
BF = jnp.bfloat16
F32 = jnp.float32
NY, NZ, NX = 2, 8, 4
TPN = 8
TA = 3
TB = TPN - TA
FC = 64
TILE = 128
ROWS = TPN * TILE
SLOTS = 256
UNROLL = 8
ANY = pl.BlockSpec(memory_space=pl.ANY)
VMEM = pl.BlockSpec(memory_space=pltpu.VMEM)
SMEM = pl.BlockSpec(memory_space=pltpu.SMEM)
NEAR_FIRST = ((0,), (1, 7), (2, 6), (3, 5), (4,))


def place():
    node, feat = lax.axis_index("node"), lax.axis_index("feat")
    return node // (NZ * NX), lax.rem(node // NX, NZ), lax.rem(node, NX), feat


def node_of(y, z, x):
    return (y * NZ + z) * NX + x


def across(feat):
    return lax.rem(feat + 2, 4)


def sibling(feat):
    return feat + 1 - 2 * lax.rem(feat, 2)


def meet(peers):
    barrier = pltpu.get_barrier_semaphore()
    for peer in peers:
        pl.semaphore_signal(barrier, inc=1, device_id=peer, device_id_type=MESH)
    pl.semaphore_wait(barrier, len(peers))


def remote(src, dst, send, recv, peer):
    return pltpu.make_async_remote_copy(
        src_ref=src, dst_ref=dst, send_sem=send, recv_sem=recv, device_id=peer, device_id_type=MESH
    )


def feat_gather(mine, full, feat, node, sems, send, recv):
    one, two = (node, across(feat)), (node, sibling(feat))
    a = remote(mine, full.at[feat], send.at[sems], recv.at[sems], one)
    b = remote(mine, full.at[feat], send.at[sems + 1], recv.at[sems + 1], two)
    a.start()
    b.start()

    def step():
        far = across(feat)
        remote(full.at[far], full.at[far], send.at[sems], recv.at[sems], one).wait_recv()
        c = remote(full.at[far], full.at[far], send.at[sems + 2], recv.at[sems + 2], two)
        c.start()

        def finish():
            near = sibling(feat)
            diag = across(near)
            remote(full.at[near], full.at[near], send.at[sems + 1], recv.at[sems + 1], two).wait_recv()
            remote(full.at[diag], full.at[diag], send.at[sems + 2], recv.at[sems + 2], two).wait_recv()
            a.wait_send()
            b.wait_send()
            c.wait_send()

        return finish

    return step


def gather_kernel(own, xown, wown, full, xfull, wfull,
                  bzs, bzr, bxs, bxr, axs, axr, azs, azr, ys, yr, fs, fr, ls):
    y, z, x, feat = place()
    node = node_of(y, z, x)
    oy = 1 - y

    def zof(k):
        return lax.rem(z + k + 2 * NZ, NZ)

    def xof(k):
        return lax.rem(x + k + 2 * NX, NX)

    def yof(j):
        return y + j - 2 * j * y

    def zdev(s):
        return (node_of(y, zof(s), x), feat)

    def xdev(s):
        return (node_of(y, z, xof(s)), feat)

    ydev = (node_of(oy, z, x), feat)
    meet([zdev(1), zdev(-1), xdev(1), xdev(-1), ydev, (node, across(feat)), (node, sibling(feat))])

    def slab(ref, lead, part, half):
        t = pl.ds(0, TA) if part == 0 else pl.ds(TA, TB)
        if half is None:
            return ref.at[(*lead, t)]
        return ref.at[(*lead, t, pl.ds(half * (FC // 2), FC // 2))]

    def move(j, zr, xr, part, s, half, send, recv, dev):
        lead = (yof(j), zof(zr), xof(xr))
        dst = slab(full, lead, part, half)
        return remote(dst, dst, send, recv, dev)

    def h(s, last):
        return (0 if s > 0 else 1) if last else None

    def bz(s, j, d, arriving=False):
        i = (0 if s > 0 else 1, j, d - 1)
        zr = -s * d if arriving else -s * (d - 1)
        return move(j, zr, 0, 1, s, h(s, d == 4), bzs.at[i], bzr.at[i], zdev(s))

    def bx(s, j, zr, d, arriving=False):
        i = (0 if s > 0 else 1, j, lax.rem(zr + NZ, NZ), d - 1)
        xr = -s * d if arriving else -s * (d - 1)
        return move(j, zr, xr, 1, s, h(s, d == 2), bxs.at[i], bxr.at[i], xdev(s))

    def ax(s, j, d, arriving=False):
        i = (0 if s > 0 else 1, j, d - 1)
        xr = -s * d if arriving else -s * (d - 1)
        return move(j, 0, xr, 0, s, h(s, d == 2), axs.at[i], axr.at[i], xdev(s))

    def az(s, j, xr, d, arriving=False):
        i = (0 if s > 0 else 1, j, lax.rem(xr + NX, NX), d - 1)
        zr = -s * d if arriving else -s * (d - 1)
        return move(j, zr, xr, 0, s, h(s, d == 4), azs.at[i], azr.at[i], zdev(s))

    local = pltpu.make_async_copy(own, full.at[y, z, x], ls.at[0])
    local.start()
    yput = remote(own, full.at[y, z, x], ys.at[0], yr.at[0], ydev)
    yput.start()
    local.wait()
    both = (1, -1)
    for j in range(2):
        if j == 1:
            remote(own, full.at[oy, z, x], ys.at[0], yr.at[0], ydev).wait_recv()
        for s in both:
            ax(s, j, 1).start()
            bz(s, j, 1).start()
        for s in both:
            bx(s, j, 0, 1).start()
            az(s, j, 0, 1).start()
        if j == 0:
            xlocal = pltpu.make_async_copy(xown, xfull.at[feat], ls.at[1])
            xlocal.start()
            wlocal = pltpu.make_async_copy(wown, wfull.at[feat], ls.at[2])
            wlocal.start()
            xstep = feat_gather(xown, xfull, feat, node, 0, fs, fr)
            wstep = feat_gather(wown, wfull, feat, node, 3, fs, fr)
    for j in range(2):
        for s in both:
            ax(s, j, 1, True).wait_recv()
        for s in both:
            az(s, j, -1, 1).start()
            az(s, j, 1, 1).start()
            ax(s, j, 2).start()
    for j in range(2):
        for s in both:
            ax(s, j, 2, True).wait_recv()
        for s in both:
            az(s, j, 2, 1).start()
    xfinish, wfinish = xstep(), wstep()

    for d in range(1, 5):
        for j in range(2):
            for s in both:
                bz(s, j, d, True).wait_recv()
                if d < 4:
                    bz(s, j, d + 1).start()
            for s in both:
                if d < 4:
                    bx(s, j, -d, 1).start()
                    bx(s, j, d, 1).start()
                else:
                    bx(s, j, 4, 1).start()

        def aunit(k, _, d=d):
            j, xr = k // NX, lax.rem(k, NX)
            for s in both:
                az(s, j, xr, d, True).wait_recv()
                if d < 4:
                    az(s, j, xr, d + 1).start()
            return 0

        lax.fori_loop(0, 2 * NX, aunit, 0)
        for j in range(2):
            for zr in sorted({-(d - 1), d - 1}):
                for s in both:
                    bx(s, j, zr, 1, True).wait_recv()
                    bx(s, j, zr, 2).start()
    for j in range(2):
        for s in both:
            bx(s, j, 4, 1, True).wait_recv()
            bx(s, j, 4, 2).start()
    for j in range(2):
        def xunit(zr, _, j=j):
            for s in both:
                bx(s, j, zr, 2, True).wait_recv()
                for d in (1, 2):
                    bx(s, j, zr, d).wait_send()
            return 0

        lax.fori_loop(0, NZ, xunit, 0)

        def zunit(xr, _, j=j):
            for s in both:
                for d in range(1, 5):
                    az(s, j, xr, d).wait_send()
            return 0

        lax.fori_loop(0, NX, zunit, 0)
        for s in both:
            for d in range(1, 5):
                bz(s, j, d).wait_send()
            for d in (1, 2):
                ax(s, j, d).wait_send()
    xfinish()
    wfinish()
    xlocal.wait()
    wlocal.wait()
    yput.wait_send()


def gather(own, xown, wown):
    dma = pltpu.SemaphoreType.DMA
    return pl.pallas_call(
        gather_kernel,
        out_shape=(
            jax.ShapeDtypeStruct((NY, NZ, NX, TPN, FC, TILE), BF),
            jax.ShapeDtypeStruct((4, *xown.shape), BF),
            jax.ShapeDtypeStruct((4, *wown.shape), BF),
        ),
        in_specs=[ANY] * 3,
        out_specs=(ANY,) * 3,
        scratch_shapes=[
            dma((2, 2, 4)), dma((2, 2, 4)), dma((2, 2, NZ, 2)), dma((2, 2, NZ, 2)),
            dma((2, 2, 2)), dma((2, 2, 2)), dma((2, 2, NX, 4)), dma((2, 2, NX, 4)),
            dma((1,)), dma((1,)), dma((6,)), dma((6,)), dma((3,)),
        ],
        compiler_params=pltpu.CompilerParams(collective_id=0, has_side_effects=True),
        name="gather",
    )(own, xown, wown)


def planes_of(words):
    return jnp.concatenate(
        [jnp.bitwise_and(jnp.right_shift(words, b), 1).astype(F32) for b in range(8)], axis=0
    )


def live_words(edges, slot, count):
    return edges[slot] * (slot < count).astype(jnp.int32)


def forward_kernel(rows, cols, count, edges, full, avg, deg, acc, cnt):
    acc[...] = jnp.zeros_like(acc)
    cnt[...] = jnp.zeros_like(cnt)
    limit = count[0]

    def group(g, _):
        for u in range(UNROLL):
            slot = g * UNROLL + u
            planes = planes_of(live_words(edges, slot, limit))
            part = jnp.dot(full[cols[slot]], planes.astype(BF), preferred_element_type=F32)
            row = rows[slot]
            acc[row] += part
            cnt[row] += jnp.sum(planes.reshape(16, 8, TILE), axis=0)
        return 0

    lax.fori_loop(0, SLOTS // UNROLL, group, 0)
    for r in range(TPN):
        degree = jnp.maximum(jnp.sum(cnt[r], axis=0, keepdims=True), 1.0)
        deg[:, r * TILE:(r + 1) * TILE] = degree
        avg[:, r * TILE:(r + 1) * TILE] = (acc[r] / degree).astype(BF)


def forward(rows, cols, count, edges, full):
    return pl.pallas_call(
        forward_kernel,
        out_shape=(
            jax.ShapeDtypeStruct((FC, ROWS), BF),
            jax.ShapeDtypeStruct((1, ROWS), F32),
        ),
        in_specs=[SMEM, SMEM, SMEM, VMEM, VMEM],
        out_specs=(VMEM, VMEM),
        scratch_shapes=[pltpu.VMEM((TPN, FC, TILE), F32), pltpu.VMEM((TPN, 8, TILE), F32)],
        compiler_params=pltpu.CompilerParams(vmem_limit_bytes=40 * 2**20),
        name="forward_sums",
    )(rows, cols, count, edges, full)


def nt(a, b):
    return lax.dot_general(a, b, (((1,), (1,)), ((), ())), preferred_element_type=F32)


def dense_kernel(avg, xfull, wfull, wself, wneigh, deg, cot, act, direct, scaled, wgrad,
                 av, gr, send, recv):
    y, z, x, feat = place()
    node = node_of(y, z, x)
    meet([(node, across(feat)), (node, sibling(feat))])
    av[feat] = avg[...]
    step = feat_gather(avg, av, feat, node, 0, send, recv)
    off = pl.multiple_of(feat * FC, FC)

    def cols_of(k, which):
        return wfull[k, pl.ds(which * 256 + off, FC), :]

    def dot(a, b):
        return jnp.dot(a, b, preferred_element_type=F32)

    pre = dot(cols_of(0, 0), xfull[0])
    for k in range(1, 4):
        pre += dot(cols_of(k, 0), xfull[k])
    step()()
    for k in range(4):
        pre += dot(cols_of(k, 1), av[k])
    sig = jax.nn.sigmoid(pre)
    act[...] = pre * sig
    grad = cot[...] * sig * (1.0 + pre * (1.0 - sig))
    gr[feat] = grad.astype(BF)
    step = feat_gather(gr.at[feat], gr, feat, node, 3, send, recv)
    step()()
    sums = dot(wneigh[:, 0:FC], gr[0])
    straight = dot(wself[:, 0:FC], gr[0])
    for k in range(1, 4):
        sums += dot(wneigh[:, k * FC:(k + 1) * FC], gr[k])
        straight += dot(wself[:, k * FC:(k + 1) * FC], gr[k])
    direct[...] = straight
    sums = (sums / deg[...]).astype(BF)
    for r in range(TPN):
        scaled[r] = sums[:, r * TILE:(r + 1) * TILE]
    mine = xfull[feat]
    for k in range(4):
        wgrad[0:FC, k * FC:(k + 1) * FC] = nt(mine, gr[k])
        wgrad[FC:2 * FC, k * FC:(k + 1) * FC] = nt(avg[...], gr[k])


def dense(avg, xfull, wfull, wself, wneigh, deg, cot):
    dma = pltpu.SemaphoreType.DMA
    return pl.pallas_call(
        dense_kernel,
        out_shape=(
            jax.ShapeDtypeStruct((FC, ROWS), F32),
            jax.ShapeDtypeStruct((FC, ROWS), F32),
            jax.ShapeDtypeStruct((TPN, FC, TILE), BF),
            jax.ShapeDtypeStruct((2 * FC, 4 * FC), F32),
        ),
        in_specs=[VMEM] * 7,
        out_specs=(VMEM,) * 4,
        scratch_shapes=[
            pltpu.VMEM((4, FC, ROWS), BF), pltpu.VMEM((4, FC, ROWS), BF), dma((6,)), dma((6,)),
        ],
        compiler_params=pltpu.CompilerParams(
            collective_id=1, has_side_effects=True, vmem_limit_bytes=40 * 2**20
        ),
        name="dense",
    )(avg, xfull, wfull, wself, wneigh, deg, cot)


def backward_kernel(rows, cols, count, edges, source, out, acc):
    acc[...] = jnp.zeros_like(acc)
    limit = count[0]

    def group(g, _):
        for u in range(UNROLL):
            slot = g * UNROLL + u
            mask = planes_of(live_words(edges, slot, limit)).astype(BF)
            part = nt(source[rows[slot]], mask)
            acc[cols[slot]] += part
        return 0

    lax.fori_loop(0, SLOTS // UNROLL, group, 0)

    def narrow(i, _):
        out[pl.ds(i * 8, 8)] = acc[pl.ds(i * 8, 8)].astype(BF)
        return 0

    lax.fori_loop(0, acc.shape[0] // 8, narrow, 0)


def backward(rows, cols, count, edges, source):
    tiles = NY * NZ * NX * TPN
    return pl.pallas_call(
        backward_kernel,
        out_shape=jax.ShapeDtypeStruct((tiles, FC, TILE), BF),
        in_specs=[SMEM, SMEM, SMEM, VMEM, VMEM],
        out_specs=VMEM,
        scratch_shapes=[pltpu.VMEM((tiles, FC, TILE), F32)],
        compiler_params=pltpu.CompilerParams(vmem_limit_bytes=48 * 2**20),
        name="backward_sums",
    )(rows, cols, count, edges, source)


def scatter_kernel(part, wgrad, out, wout,
                   rbx, rbz, rax, raz, ry, w1, w2,
                   bzs, bzr, bxs, bxr, axs, axr, azs, azr, ys, yr, ws, wr):
    y, z, x, feat = place()
    oy = 1 - y

    def zof(k):
        return lax.rem(z + k + 2 * NZ, NZ)

    def xof(k):
        return lax.rem(x + k + 2 * NX, NX)

    def yof(j):
        return y + j - 2 * j * y

    def zdev(s):
        return (node_of(y, zof(s), x), feat)

    def xdev(s):
        return (node_of(y, z, xof(s)), feat)

    plane = y * NX + x

    def pof(k):
        return lax.rem(plane + k, NY * NX)

    def pdev(k):
        p = pof(k)
        return (node_of(p // NX, z, lax.rem(p, NX)), feat)

    meet([zdev(k) for k in range(1, NZ)] + [pdev(k) for k in range(1, NY * NX)])
    ydev = (node_of(oy, z, x), feat)

    PA, PB = pl.ds(0, TA), pl.ds(TA, TB)
    both = (1, -1)

    def di(s):
        return 0 if s > 0 else 1

    def cut(half):
        return pl.ds(half * (FC // 2), FC // 2)

    def hop(buf, i, d, last, half, src, send, recv, dev):
        if d == last:
            return remote(src.at[:, cut(half)], buf.at[i].at[:, cut(half)], send.at[i], recv.at[i], dev)
        return remote(src, buf.at[i], send.at[i], recv.at[i], dev)

    def bx(s, j, zr, d):
        i = (di(s), j, lax.rem(zr + NZ, NZ), d - 1)
        src = part.at[yof(j), zof(zr), xof(2 * s), PB] if d == 2 else rbx.at[di(s), j, lax.rem(zr + NZ, NZ), 1]
        return hop(rbx, i, d, 2, di(s), src, bxs, bxr, xdev(s))

    def az(s, j, xr, d):
        i = (di(s), j, lax.rem(xr + NX, NX), d - 1)
        src = part.at[yof(j), zof(4 * s), xof(xr), PA] if d == 4 else raz.at[di(s), j, lax.rem(xr + NX, NX), d]
        return hop(raz, i, d, 4, di(s), src, azs, azr, zdev(s))

    def bz(s, j, d):
        i = (di(s), j, d - 1)
        src = rbx.at[0, j, 4, 0] if d == 4 else rbz.at[di(s), j, d]
        return hop(rbz, i, d, 4, di(s), src, bzs, bzr, zdev(s))

    def ax(s, j, d):
        i = (di(s), j, d - 1)
        src = raz.at[0, j, 2, 0] if d == 2 else rax.at[di(s), j, 1]
        return hop(rax, i, d, 2, di(s), src, axs, axr, xdev(s))

    def add(buf, i, term, first, s):
        if first:
            a, b = cut(di(s)), cut(1 - di(s))
            buf[(*i, slice(None), a)] = (
                buf[(*i, slice(None), a)].astype(F32) + term[:, a].astype(F32)
            ).astype(BF)
            buf[(*i, slice(None), b)] = term[:, b]
        else:
            buf[i] = (buf[i].astype(F32) + term[...].astype(F32)).astype(BF)

    def total(buf, i, term):
        one, two = (0, *i, 0), (1, *i, 0)
        buf[one] = (buf[one].astype(F32) + buf[two].astype(F32) + term[...].astype(F32)).astype(BF)

    def bx_first(j, zr):
        for s in both:
            bx(s, j, zr, 2).start()

    def bx_next(j, zr):
        r = lax.rem(zr + NZ, NZ)
        for s in both:
            bx(s, j, zr, 2).wait_recv()
            add(rbx, (di(s), j, r, 1), part.at[yof(j), zof(zr), xof(s), PB], True, s)
            bx(s, j, zr, 1).start()

    def bx_last(j, zr):
        r = lax.rem(zr + NZ, NZ)
        for s in both:
            bx(s, j, zr, 1).wait_recv()
        total(rbx, (j, r), part.at[yof(j), zof(zr), x, PB])

    def az_next(d):
        def unit(k, _):
            j, xr = 1 - k // NX, lax.rem(k + 2, NX)
            for s in both:
                az(s, j, xr, d).wait_recv()
                add(raz, (di(s), j, xr, d - 1), part.at[yof(j), zof(s * (d - 1)), xof(xr), PA], d == 4, s)
                az(s, j, xr, d - 1).start()
            return 0

        lax.fori_loop(0, 2 * NX, unit, 0)

    def bz_next(d):
        for j in (1, 0):
            for s in both:
                bz(s, j, d).wait_recv()
                add(rbz, (di(s), j, d - 1), rbx.at[0, j, lax.rem(s * (d - 1) + NZ, NZ), 0], d == 4, s)
                bz(s, j, d - 1).start()

    def wcopy(phase, k):
        i = phase * 7 + k - 1
        if phase == 0:
            return remote(wgrad.at[pl.ds(pl.multiple_of(zof(k) * 16, 16), 16)], w1.at[k - 1], ws.at[i], wr.at[i], zdev(k))
        if phase == 1:
            return remote(w2.at[plane], w2.at[plane], ws.at[i], wr.at[i], pdev(k))
        rows = pl.ds(pl.multiple_of(z * 16, 16), 16)
        return remote(wout.at[rows], wout.at[rows], ws.at[i], wr.at[i], zdev(k))

    def wexpect(phase, k):
        i = phase * 7 + k - 1
        if phase == 0:
            dst = w1.at[k - 1]
        elif phase == 1:
            dst = w2.at[lax.rem(plane + NY * NX - k, NY * NX)]
        else:
            dst = wout.at[pl.ds(pl.multiple_of(zof(-k) * 16, 16), 16)]
        return remote(dst, dst, ws.at[i], wr.at[i], zdev(k))

    def units(r):
        return NEAR_FIRST[4 - r]

    for r in range(2):
        for j in (1, 0):
            for zr in units(r):
                bx_first(j, zr)
        if r == 0:
            def begin(k, _):
                j, xr = 1 - k // NX, lax.rem(k + 2, NX)
                for s in both:
                    az(s, j, xr, 4).start()
                return 0

            lax.fori_loop(0, 2 * NX, begin, 0)
            for k in range(1, NZ):
                wcopy(0, k).start()
    for r in range(6):
        if r < 5:
            for j in (1, 0):
                for zr in units(r):
                    bx_next(j, zr)
                if r + 2 < 5:
                    for zr in units(r + 2):
                        bx_first(j, zr)
        if r >= 1:
            for j in (1, 0):
                for zr in units(r - 1):
                    bx_last(j, zr)
        if r == 1:
            for j in (1, 0):
                for s in both:
                    bz(s, j, 4).start()
        if 2 <= r <= 4:
            bz_next(6 - r)
        if r <= 2:
            az_next(4 - r)
        if r == 0:
            for k in range(1, NZ):
                wexpect(0, k).wait_recv()
            acc = wgrad[pl.ds(pl.multiple_of(z * 16, 16), 16)]
            for k in range(1, NZ):
                acc += w1[k - 1]
            w2[plane] = acc
            for k in range(1, NY * NX):
                wcopy(1, k).start()
        if r == 2:
            for k in range(1, NY * NX):
                wexpect(1, k).wait_recv()
            acc = w2[0]
            for k in range(1, NY * NX):
                acc += w2[k]
            wout[pl.ds(pl.multiple_of(z * 16, 16), 16)] = acc
            for k in range(1, NZ):
                wcopy(2, k).start()
        if r == 3:
            def alast(k, _):
                j, xr = 1 - k // NX, lax.rem(k + 2, NX)
                for s in both:
                    az(s, j, xr, 1).wait_recv()
                total(raz, (j, xr), part.at[yof(j), z, xof(xr), PA])
                return 0

            lax.fori_loop(0, 2 * NX, alast, 0)
            for j in (1, 0):
                for s in both:
                    ax(s, j, 2).start()
        if r == 4:
            for j in (1, 0):
                for s in both:
                    ax(s, j, 2).wait_recv()
                    add(rax, (di(s), j, 1), raz.at[0, j, lax.rem(s + NX, NX), 0], True, s)
                    ax(s, j, 1).start()
        if r == 5:
            for j in (1, 0):
                for s in both:
                    bz(s, j, 1).wait_recv()
                    ax(s, j, 1).wait_recv()
                total(rbz, (j,), rbx.at[0, j, 0, 0])
                total(rax, (j,), raz.at[0, j, 0, 0])
                if j == 1:
                    aput = remote(rax.at[0, 1, 0], ry.at[PA], ys.at[0], yr.at[0], ydev)
                    bput = remote(rbz.at[0, 1, 0], ry.at[PB], ys.at[1], yr.at[1], ydev)
                    aput.start()
                    bput.start()
    aput.wait_recv()
    bput.wait_recv()
    out[PA] = rax[0, 0, 0].astype(F32) + ry[PA].astype(F32)
    out[PB] = rbz[0, 0, 0].astype(F32) + ry[PB].astype(F32)

    for k in range(1, NZ):
        wexpect(2, k).wait_recv()
    for j in range(2):
        def xunit(zr, _, j=j):
            for s in both:
                for d in (1, 2):
                    bx(s, j, zr, d).wait_send()
            return 0

        lax.fori_loop(0, NZ, xunit, 0)

        def zunit(xr, _, j=j):
            for s in both:
                for d in range(1, 5):
                    az(s, j, xr, d).wait_send()
            return 0

        lax.fori_loop(0, NX, zunit, 0)
        for s in both:
            for d in range(1, 5):
                bz(s, j, d).wait_send()
            for d in (1, 2):
                ax(s, j, d).wait_send()
    aput.wait_send()
    bput.wait_send()
    for phase in range(3):
        for k in range(1, 8):
            wcopy(phase, k).wait_send()


def scatter(part, wgrad):
    dma = pltpu.SemaphoreType.DMA
    return pl.pallas_call(
        scatter_kernel,
        out_shape=(
            jax.ShapeDtypeStruct((TPN, FC, TILE), F32),
            jax.ShapeDtypeStruct(wgrad.shape, F32),
        ),
        in_specs=[VMEM, VMEM],
        out_specs=(VMEM, VMEM),
        scratch_shapes=[
            pltpu.VMEM((2, 2, NZ, 2, TB, FC, TILE), BF),
            pltpu.VMEM((2, 2, 4, TB, FC, TILE), BF),
            pltpu.VMEM((2, 2, 2, TA, FC, TILE), BF),
            pltpu.VMEM((2, 2, NX, 4, TA, FC, TILE), BF),
            pltpu.VMEM((TPN, FC, TILE), BF),
            pltpu.VMEM((NZ - 1, 16, 256), F32),
            pltpu.VMEM((NY * NX, 16, 256), F32),
            dma((2, 2, 4)), dma((2, 2, 4)), dma((2, 2, NZ, 2)), dma((2, 2, NZ, 2)),
            dma((2, 2, 2)), dma((2, 2, 2)), dma((2, 2, NX, 4)), dma((2, 2, NX, 4)),
            dma((2,)), dma((2,)), dma((21,)), dma((21,)),
        ],
        compiler_params=pltpu.CompilerParams(
            collective_id=2, has_side_effects=True, vmem_limit_bytes=48 * 2**20
        ),
        name="scatter",
    )(part, wgrad)


def local(features, w_self, w_neigh, tile_rows, tile_cols, tile_count, edge_bits, cotangent):
    own = features.reshape(TPN, TILE // 8, 8, FC).transpose(0, 3, 2, 1).reshape(TPN, FC, TILE)
    wt = jnp.concatenate([w_self.T, w_neigh.T], axis=0)
    full, xfull, wfull = gather(own, features.T, wt)
    avg, deg = forward(tile_rows, tile_cols, tile_count, edge_bits, full.reshape(-1, FC, TILE))
    act, direct, scaled, wgrad = dense(avg, xfull, wfull, w_self, w_neigh, deg, cotangent.T)
    part = backward(tile_rows, tile_cols, tile_count, edge_bits, scaled)
    back, wsum = scatter(part.reshape(NY, NZ, NX, TPN, FC, TILE), wgrad)
    back = back.reshape(TPN, FC, 8, TILE // 8).transpose(0, 3, 2, 1).reshape(ROWS, FC)
    return act.T, direct.T + back, wsum[:FC], wsum[FC:]


def solution(mesh):
    placed = (
        P("node", "feat"),
        P("feat", None),
        P("feat", None),
        P("node"),
        P("node"),
        P("node"),
        P("node", None, None),
        P("node", "feat"),
    )
    return jax.shard_map(
        local,
        mesh=mesh,
        in_specs=placed,
        out_specs=(P("node", "feat"), P("node", "feat"), P("feat", None), P("feat", None)),
        check_vma=False,
    )
```

time: 1360 us -> 185 us (0.14)
  waiting for transfers between devices: 1190 us -> 0 us
  Pallas kernels: 0 us -> 170 us
  matrix products: 60.6 us -> 0 us
  other arithmetic: 47.2 us -> 1.42 us
  local copies, waits for them, and re-layouts: 43.5 us -> 11.9 us
    psum x1 -> x0, waiting for transfers between devices: 606 us -> none  [local(): grad_self, grad_neigh = lax.psum((part_self, part_neigh), 'node')]
    reduce_scatter x2 -> x0, waiting for transfers between devices: 418 us -> none  [the longest x1 397 us: local(): lax.psum_scatter(accum.reshape(all_tiles * tile_size, feat_cols), 'node',...]
    pallas_call x0 -> x5, Pallas kernels: none -> 170 us  [the longest x1 66.6 us: gather(): pl.pallas_call(gather_kernel, out_shape=(jax.ShapeDtypeStruct((NY, NZ, NX...]
    all_gather x2 -> x0, waiting for transfers between devices: 169 us -> none  [the longest x1 144 us: local(): gathered = lax.all_gather(features, 'node', axis=0, tiled=True)]
    dot_general x10 -> x0, matrix products: 60.6 us -> none  [the longest x1 37.2 us: local(): contrib = jnp.einsum('tqp,tpf->tqf', mask_f32, source, precision=hi)]
    scatter-add x1 -> x0, other arithmetic: 39.4 us -> none  [local(): jnp.zeros((all_tiles, tile_size, feat_cols), jnp.float32).at[tile_cols]]
    reshape x3 -> x2, local copies, waits for them, and re-layouts: 20.4 us -> 0.97 us  [the longest x1 0.79 us: local(): features.reshape(TPN, TILE // 8, 8, FC).transpose(0, 3, 2, 1)]
  transfers between devices with their start and end apart: 5 -> 0, of which waited for: 5 -> 0; matrix products, arithmetic and copies ran while one was open for 1% -> 0% of each run, Pallas kernels for 0% -> 0%
where the time goes in v1:
time: 185 us
  Pallas kernels  170 us (92%)
  local copies, waits for them, and re-layouts  11.9 us (6%)
    pallas_call x1, Pallas kernels, gather(): pl.pallas_call(gather_kernel, out_shape=(jax.ShapeDtypeStruct((NY, NZ, NX...  66.6 us
    pallas_call x1, Pallas kernels, scatter(): pl.pallas_call(scatter_kernel, out_shape=(jax.ShapeDtypeStruct((TPN, FC,...  66.5 us
    pallas_call x1, Pallas kernels, backward(): pl.pallas_call(backward_kernel, out_shape=jax.ShapeDtypeStruct((tiles, FC...  15.4 us
    pallas_call x1, Pallas kernels, dense(): pl.pallas_call(dense_kernel, out_shape=(jax.ShapeDtypeStruct((FC, ROWS),...  13.6 us
    unnamed x22, local copies, waits for them, and re-layouts  9.91 us
    pallas_call x1, Pallas kernels, forward(): pl.pallas_call(forward_kernel, out_shape=(jax.ShapeDtypeStruct((FC, ROWS)...  7.62 us

profile of v1, /device:TPU:24, one launch (start us, length us, event | category | flops | bytes accessed | tf_op | source)
XLA Modules:
  0.0 184.5 jit_solution(12637846784914711634)
XLA Ops:
  0.6 0.0 copy-start.6
  0.6 0.0 copy-start.5
  0.7 0.0 copy-start.4
  0.7 1.1 copy.16
  1.8 0.8 copy.20.own
  2.6 0.9 copy.18
  3.5 0.9 copy.19
  4.4 0.7 pad_maximum_fusion.wown
  5.1 66.6 %gather.1 = (bf16[2,8,4,8,64,128]{5,4,3,2,1,0:T(8,128)(2,1)}, bf16[4,64,1024]{2,1,0:T(8,128)(2,1)}, bf16[4,512,64]{2,1,0:T(8,128)(2,1)}) custom-call(bf16[8,64,128]{2,1,0:T(8,128)(2,1)} %copy.20.own, bf16[64,1024]{1,0:T(8,128)(2,1)} %bitcast.25, bf16[512,64]{1,0:T(8,128)(2,1)} %pad_maximum_fusion.wown), custom_call_target="tpu_custom_call" | custom-call | tf_op jit(solution)/shard_map/gather/pallas_call | solution.py:239
  72.3 0.0 copy-start
  72.3 3.4 %copy-done = bf16[2,8,4,8,64,128]{5,4,3,2,1,0:T(8,128)(2,1)S(1)} copy-done((bf16[2,8,4,8,64,128]{5,4,3,2,1,0:T(8,128)(2,1)S(1)}, bf16[2,8,4,8,64,128]{5,4,3,2,1,0:T(8,128)(2,1)}, u32[]{:S(2)}) %copy-start) | copy-done | bytes 8388632
  75.7 0.0 copy-start.1
  75.7 1.6 copy-done.1
  77.3 0.0 copy-start.7
  77.3 0.7 copy-done.7
  78.0 0.0 copy-start.8
  78.0 0.7 copy-done.8
  78.6 7.6 %forward_sums.1 = (bf16[64,1024]{1,0:T(8,128)(2,1)S(1)}, f32[1,1024]{1,0:T(1,128)S(1)}) custom-call(s32[256]{0:T(256)S(1)} %copy-done.7, s32[256]{0:T(256)S(1)} %copy-done.8, s32[1]{0:T(128)S(6)} %copy.25.count, s32[256,16,128]{2,1,0:T(8,128)S(1)} %copy-done.1, bf16[512,64,128]{2,1,0:T(8,128)(2,1)S(1)} %bitcast.17), custom_call_target="tpu_custom_call" | custom-call | tf_op jit(solution)/shard_map/forward_sums/pallas_call | solution.py:291
  86.3 0.0 copy-done.6
  86.3 0.0 copy-done.5
  86.3 0.0 copy-done.4
  86.3 0.0 copy-done.2
  86.3 0.0 copy-done.3
  86.3 13.6 %dense.1 = (f32[64,1024]{1,0:T(8,128)S(1)}, f32[64,1024]{1,0:T(8,128)S(1)}, bf16[8,64,128]{2,1,0:T(8,128)(2,1)S(1)}, f32[128,256]{1,0:T(8,128)S(1)}) custom-call(bf16[64,1024]{1,0:T(8,128)(2,1)S(1)} %get-tuple-element.16.avg, bf16[4,64,1024]{2,1,0:T(8,128)(2,1)S(1)} %copy-done.2, bf16[4,512,64]{2,1,0:T(8,128)(2,1)S(1)} %copy-done.3, ...), custom_call_target="tpu_custom_call" | custom-call | tf_op jit(solution)/shard_map/dense/pallas_call | solution.py:353
  99.9 15.4 %backward_sums.1 = bf16[512,64,128]{2,1,0:T(8,128)(2,1)} custom-call(s32[256]{0:T(256)S(1)} %copy-done.7, s32[256]{0:T(256)S(1)} %copy-done.8, s32[1]{0:T(128)S(6)} %copy.25.count, s32[256,16,128]{2,1,0:T(8,128)S(1)} %copy-done.1, bf16[8,64,128]{2,1,0:T(8,128)(2,1)S(1)} %get-tuple-element.22.source), custom_call_target="tpu_custom_call" | custom-call | tf_op jit(solution)/shard_map/backward_sums/pallas_call | solution.py:396
  115.4 66.5 %scatter.1 = (f32[8,64,128]{2,1,0:T(8,128)S(1)}, f32[128,256]{1,0:T(8,128)S(1)}) custom-call(bf16[2,8,4,8,64,128]{5,4,3,2,1,0:T(8,128)(2,1)} %bitcast.20, f32[128,256]{1,0:T(8,128)S(1)} %get-tuple-element.23.wgrad), custom_call_target="tpu_custom_call" | custom-call | tf_op jit(solution)/shard_map/scatter/pallas_call | solution.py:664
  181.9 0.2 copy.21
  182.1 0.2 copy.22
  182.2 0.2 copy.23
  182.4 0.7 bitcast_add_fusion
  183.2 0.7 fusion
  183.8 0.7 copy.26
  (3 shorter events, 0.0 us)
Async XLA Ops:
  0.6 85.6 %copy-start.6 = (bf16[64,256]{1,0:T(8,128)(2,1)S(1)}, bf16[64,256]{1,0:T(8,128)(2,1)}, u32[]{:S(2)}) copy-start(bf16[64,256]{1,0:T(8,128)(2,1)} %wself.1) | copy-start | bytes 98308
  0.6 85.6 %copy-start.5 = (bf16[64,256]{1,0:T(8,128)(2,1)S(1)}, bf16[64,256]{1,0:T(8,128)(2,1)}, u32[]{:S(2)}) copy-start(bf16[64,256]{1,0:T(8,128)(2,1)} %wneigh.1) | copy-start | bytes 98308
  0.7 85.6 %copy-start.4 = (f32[1024,64]{0,1:T(8,128)S(1)}, f32[1024,64]{0,1:T(8,128)}, u32[]{:S(2)}) copy-start(f32[1024,64]{0,1:T(8,128)} %param.15) | copy-start | bytes 786436
  72.3 3.4 %copy-start = (bf16[2,8,4,8,64,128]{5,4,3,2,1,0:T(8,128)(2,1)S(1)}, bf16[2,8,4,8,64,128]{5,4,3,2,1,0:T(8,128)(2,1)}, u32[]{:S(2)}) copy-start(bf16[2,8,4,8,64,128]{5,4,3,2,1,0:T(8,128)(2,1)} %get-tuple-element.15) | copy-start | bytes 25165828
  75.7 1.6 copy-start.1
  77.3 0.7 copy-start.7
  78.0 0.7 copy-start.8
  78.6 7.7 %copy-start.2 = (bf16[4,64,1024]{2,1,0:T(8,128)(2,1)S(1)}, bf16[4,64,1024]{2,1,0:T(8,128)(2,1)}, u32[]{:S(2)}) copy-start(bf16[4,64,1024]{2,1,0:T(8,128)(2,1)} %get-tuple-element.17.xfull) | copy-start | bytes 1572868
  78.6 7.7 %copy-start.3 = (bf16[4,512,64]{2,1,0:T(8,128)(2,1)S(1)}, bf16[4,512,64]{2,1,0:T(8,128)(2,1)}, u32[]{:S(2)}) copy-start(bf16[4,512,64]{2,1,0:T(8,128)(2,1)} %get-tuple-element.18.wfull) | copy-start | bytes 786436

commit v2 on v0

v2 whole, which is shorter than its diff:
```python
import jax
import jax.numpy as jnp
from jax import lax
from jax.experimental import pallas as pl
from jax.experimental.pallas import tpu as pltpu
from jax.sharding import PartitionSpec as P

MESH = pl.DeviceIdType.MESH
BF = jnp.bfloat16
F32 = jnp.float32
NY, NZ, NX = 2, 8, 4
TPN = 8
FC = 64
TILE = 128
ROWS = TPN * TILE
SLOTS = 256
WORDS = 16
CNT = 8
BOTH = (1, -1)
UNROLL = 8
ANY = pl.BlockSpec(memory_space=pl.ANY)
VMEM = pl.BlockSpec(memory_space=pltpu.VMEM)
SMEM = pl.BlockSpec(memory_space=pltpu.SMEM)
OUT = pltpu.VMEM


def place():
    node, feat = lax.axis_index("node"), lax.axis_index("feat")
    return node // (NZ * NX), lax.rem(node // NX, NZ), lax.rem(node, NX), feat


def side(s):
    return 0 if s > 0 else 1


def node_of(y, z, x):
    return (y * NZ + z) * NX + x


def across(feat):
    return lax.rem(feat + 2, 4)


def sibling(feat):
    return feat + 1 - 2 * lax.rem(feat, 2)


def meet(peers):
    barrier = pltpu.get_barrier_semaphore()
    for peer in peers:
        pl.semaphore_signal(barrier, inc=1, device_id=peer, device_id_type=MESH)
    pl.semaphore_wait(barrier, len(peers))


def remote(src, dst, send, recv, peer):
    return pltpu.make_async_remote_copy(
        src_ref=src, dst_ref=dst, send_sem=send, recv_sem=recv, device_id=peer, device_id_type=MESH
    )


def exchange(mine, slot, feat, node, sems, send, recv):
    one, two = (node, across(feat)), (node, sibling(feat))
    far, near = across(feat), sibling(feat)
    diag = across(near)
    a = remote(mine, slot(feat), send.at[sems], recv.at[sems], one)
    b = remote(mine, slot(feat), send.at[sems + 1], recv.at[sems + 1], two)
    c = remote(slot(far), slot(far), send.at[sems + 2], recv.at[sems + 2], two)
    a.start()
    b.start()

    def step():
        remote(slot(far), slot(far), send.at[sems], recv.at[sems], one).wait_recv()
        c.start()

    def finish():
        remote(slot(near), slot(near), send.at[sems + 1], recv.at[sems + 1], two).wait_recv()
        remote(slot(diag), slot(diag), send.at[sems + 2], recv.at[sems + 2], two).wait_recv()
        a.wait_send()
        b.wait_send()
        c.wait_send()

    return step, finish


def dot(a, b):
    return jnp.dot(a, b, preferred_element_type=F32)


def nt(a, b):
    return lax.dot_general(a, b, (((1,), (1,)), ((), ())), preferred_element_type=F32)


def iota(shape, dim):
    return lax.broadcasted_iota(jnp.int32, shape, dim)


def order():
    old = iota((TILE, TILE), 1)
    new = jnp.bitwise_and(old, 7) * WORDS + lax.shift_right_logical(old, 3)
    return (iota((TILE, TILE), 0) == new).astype(F32).astype(BF)


def gather_kernel(feats, wself, wneigh, rows, cols, count, words, full, xfull, wfull, edges, listed,
                  raw, wt, codes, marks,
                  zs, zr, es, er, bs, br, cs, cr, ys, yr, fs, fr, ls):
    y, z, x, feat = place()
    node = node_of(y, z, x)
    oy = 1 - y

    def zof(k):
        return lax.rem(z + k + 2 * NZ, NZ)

    def xof(k):
        return lax.rem(x + k + 2 * NX, NX)

    def yof(j):
        return y + j - 2 * j * y

    def zdev(s):
        return (node_of(y, zof(s), x), feat)

    def xdev(s):
        return (node_of(y, z, xof(s)), feat)

    ydev = (node_of(oy, z, x), feat)
    beside = (node, sibling(feat))
    peers = [zdev(1), zdev(-1), xdev(1), xdev(-1), xdev(2), ydev, (node, across(feat)), beside]
    barrier = pltpu.get_barrier_semaphore()
    for peer in peers:
        pl.semaphore_signal(barrier, inc=1, device_id=peer, device_id_type=MESH)

    half = lax.rem(feat, 2) * (SLOTS // 2)
    other = SLOTS // 2 - half
    PART = SLOTS // 8

    def load(c):
        base = half + c * PART if c < 4 else other
        span = pl.ds(base, PART if c < 4 else SLOTS // 2)
        return pltpu.make_async_copy(words.at[span], raw.at[span], ls.at[c])

    for c in range(5):
        load(c).start()
    perm = order()
    for t in range(TPN):
        full[y, z, t] = dot(perm, feats[t * TILE:(t + 1) * TILE, :]).T.astype(BF)
    pl.semaphore_wait(barrier, len(peers))

    def chunk(ref, c):
        return ref.at[pl.ds(c * (TPN // 2), TPN // 2)]

    def yhop(c, arriving=False):
        at = chunk(full.at[oy if arriving else y, z], c)
        return remote(at, at, ys.at[c], yr.at[c], ydev)

    def zhop(s, j, c, d, arriving=False):
        i = (side(s), j, c, d - 1)
        at = chunk(full.at[yof(j), zof(-s * d if arriving else -s * (d - 1))], c)
        return remote(at, at, zs.at[i], zr.at[i], zdev(s))

    def ehop(s, c, d, arriving=False):
        i = (side(s), c, d - 1)
        at = edges.at[xof(-s * d if arriving else -s * (d - 1)), pl.ds(half + c * PART, PART)]
        return remote(at, at, es.at[i], er.at[i], xdev(s))

    def ehand(s, c, d, arriving=False):
        i = (side(s), c, d - 1)
        at = edges.at[xof(-s * d), pl.ds((other if arriving else half) + c * PART, PART)]
        return remote(at, at, bs.at[i], br.at[i], beside)

    def nth(s, i):
        return i if s > 0 else (i + 2) % 4

    def chop(k, arriving=False):
        at = marks.at[xof(-k) if arriving else x]
        return remote(codes if not arriving else at, at, cs.at[k - 1], cr.at[k - 1], xdev(k))

    for c in range(2):
        yhop(c).start()
        for s in BOTH:
            zhop(s, 0, c, 1).start()
    for i in range(4):
        load(i).wait()
        span = pl.ds(half + i * PART, PART)
        edges[x, span] = raw[span].astype(jnp.int16)
        if i == 1:
            for k in (0, 1):
                ehop(1, nth(1, k), 1).start()
    for k in range(4):
        ehop(-1, nth(-1, k), 1).start()
        if k > 1:
            ehop(1, nth(1, k), 1).start()
    limit = count[0]
    at = iota((2, TILE), 0) * TILE + iota((2, TILE), 1)
    codes[...] = jnp.full_like(codes, -1)
    codes[0:2] = jnp.where(at < limit, rows[...] * 65536 + cols[...], -1)
    marks[x] = codes[...]
    for k in range(1, NX):
        chop(k).start()
    for c in range(2):
        yhop(c, True).wait_recv()
        for s in BOTH:
            zhop(s, 1, c, 1).start()
    wt[0:256] = wself[...].astype(F32).T.astype(BF)
    wt[256:512] = wneigh[...].astype(F32).T.astype(BF)
    xstep, xfinish = exchange(full.at[y, z], lambda k: xfull.at[k], feat, node, 0, fs, fr)
    wstep, wfinish = exchange(wt, lambda k: wfull.at[k], feat, node, 3, fs, fr)
    xfull[feat] = full[y, z]
    wfull[feat] = wt[...]

    def zround(d):
        for j in range(2):
            for c in range(2):
                for s in BOTH:
                    if d < 4 or c == side(s):
                        zhop(s, j, c, d, True).wait_recv()
                        if d < 3 or (d == 3 and c == side(s)):
                            zhop(s, j, c, d + 1).start()

    def eround(i):
        for s in BOTH:
            c = nth(s, i)
            ehop(s, c, 1, True).wait_recv()
            if i < 2:
                ehop(s, c, 2).start()
            ehand(s, c, 1).start()

    zround(1)
    eround(0)
    load(4).wait()
    span = pl.ds(other, SLOTS // 2)
    edges[x, span] = raw[span].astype(jnp.int16)
    for k in range(1, NX):
        chop(k, True).wait_recv()
    xstep()
    wstep()
    eround(1)
    zround(2)
    code = jnp.concatenate([marks[b, 0:2] for b in range(NX)], axis=0)
    col = jnp.bitwise_and(code, 511)
    mine = jnp.where(
        jnp.logical_and(code >= 0, jnp.bitwise_and(lax.shift_right_logical(col, 3), 3) == x), 1.0, 0.0
    )
    slot = iota((8, TILE), 0) * TILE + iota((8, TILE), 1)
    row = lax.shift_right_logical(slot, 8) * TPN + jnp.bitwise_and(lax.shift_right_arithmetic(code, 16), 7)
    near = lax.shift_left(lax.shift_right_logical(col, 5), 3) + jnp.bitwise_and(col, 7)
    upto = jnp.where(iota((TILE, TILE), 0) <= iota((TILE, TILE), 1), 1.0, 0.0).astype(BF)
    prefix = dot(mine.astype(BF), upto)
    pos = jnp.where(mine > 0.0, prefix - 1.0, -1.0e6)
    base = jnp.zeros((1, 1), F32)
    shifted = []
    for r in range(8):
        shifted.append(pos[r:r + 1] + base)
        base = base + prefix[r:r + 1, TILE - 1:TILE]
    pos = jnp.concatenate(shifted + [jnp.zeros((TILE - 8, TILE), F32)], axis=0).T
    eround(2)
    wide = iota((TILE, 8 * TILE), 1).astype(F32)
    picked = jnp.zeros((8, 8 * TILE), F32)
    fields = (jnp.bitwise_and(slot, 255), lax.shift_right_logical(slot, 8), row, near)
    for r in range(8):
        hot = jnp.where(pos[:, r:r + 1] == wide, 1.0, 0.0).astype(BF)
        stack = jnp.concatenate([f[r:r + 1].astype(F32) for f in fields] + [jnp.zeros((4, TILE), F32)], axis=0)
        picked += dot(stack.astype(BF), hot)
    items = (picked[0:1] + 256.0 * picked[1:2] + 1024.0 * picked[2:3] + 32768.0 * picked[3:4]).astype(jnp.int32)
    for r in range(8):
        listed[r:r + 1] = items[:, r * TILE:(r + 1) * TILE]
    listed[8:16] = jnp.broadcast_to(base, (8, TILE)).astype(jnp.int32)
    eround(3)
    zround(3)
    for i in range(2):
        for s in BOTH:
            c = nth(s, i)
            ehop(s, c, 2, True).wait_recv()
            ehand(s, c, 2).start()
    zround(4)
    for s in BOTH:
        for i in range(4):
            c = nth(s, i)
            for d in (1, 2) if i < 2 else (1,):
                ehand(s, c, d, True).wait_recv()
                ehand(s, c, d).wait_send()
                ehop(s, c, d).wait_send()
        for j in range(2):
            for c in range(2):
                for d in range(1, 5 if c == side(s) else 4):
                    zhop(s, j, c, d).wait_send()
    for k in range(1, NX):
        chop(k).wait_send()
    xfinish()
    wfinish()
    for c in range(2):
        yhop(c).wait_send()


def gather(feats, wself, wneigh, rows, cols, count, words):
    dma = pltpu.SemaphoreType.DMA
    return pl.pallas_call(
        gather_kernel,
        out_shape=(
            OUT((NY, NZ, TPN, FC, TILE), BF),
            OUT((4, TPN, FC, TILE), BF),
            OUT((4, 512, FC), BF),
            OUT((NX, *words.shape), jnp.int16),
            jax.ShapeDtypeStruct((16, TILE), jnp.int32),
        ),
        in_specs=[VMEM] * 5 + [SMEM, ANY],
        out_specs=(VMEM,) * 5,
        scratch_shapes=[
            pltpu.VMEM(words.shape, jnp.int32), pltpu.VMEM((512, FC), BF),
            pltpu.VMEM((8, TILE), jnp.int32), pltpu.VMEM((NX, 8, TILE), jnp.int32),
            dma((2, 2, 2, 4)), dma((2, 2, 2, 4)), dma((2, 4, 2)), dma((2, 4, 2)), dma((2, 4, 2)), dma((2, 4, 2)),
            dma((3,)), dma((3,)), dma((2,)), dma((2,)), dma((6,)), dma((6,)), dma((5,)),
        ],
        compiler_params=pltpu.CompilerParams(
            collective_id=0, has_side_effects=True, vmem_limit_bytes=24 * 2**20
        ),
        name="gather",
    )(feats, wself, wneigh, rows, cols, count, words)


def planes_of(words):
    return jnp.concatenate(
        [jnp.bitwise_and(jnp.right_shift(words, b), 1).astype(F32) for b in range(8)], axis=0
    )


def entry(slots, group, u, count, edges):
    item = slots[lax.shift_right_logical(group, 4), jnp.bitwise_and(group, 15) * UNROLL + u]
    live = (group * UNROLL + u < count).astype(jnp.int32)
    words = edges[jnp.bitwise_and(lax.shift_right_logical(item, 8), 3), jnp.bitwise_and(item, 255)]
    planes = planes_of(words.astype(jnp.int32) * live)
    return jnp.bitwise_and(lax.shift_right_logical(item, 10), 31), lax.shift_right_logical(item, 15), planes


def forward_kernel(slots, edges, full, acc):
    acc[...] = jnp.zeros_like(acc)
    count = slots[8, 0]

    def group(g, _):
        for u in range(UNROLL):
            row, col, planes = entry(slots, g, u, count, edges)
            near, t = lax.shift_right_logical(col, 3), jnp.bitwise_and(col, 7)
            block, tile = lax.shift_right_logical(row, 3), jnp.bitwise_and(row, 7)
            source = full[lax.shift_right_logical(near, 3), jnp.bitwise_and(near, 7), t]
            acc[block, tile, 0:FC] += dot(source, planes.astype(BF))
            acc[block, tile, FC:FC + CNT] += jnp.sum(planes.reshape(TILE // CNT, CNT, TILE), axis=0)
        return 0

    lax.fori_loop(0, (count + UNROLL - 1) // UNROLL, group, 0)


def forward(slots, edges, full):
    return pl.pallas_call(
        forward_kernel,
        out_shape=OUT((NX, TPN, FC + CNT, TILE), F32),
        in_specs=[SMEM, VMEM, VMEM],
        out_specs=VMEM,
        compiler_params=pltpu.CompilerParams(vmem_limit_bytes=24 * 2**20),
        name="forward_sums",
    )(slots, edges, full)


def dense_kernel(part, xfull, wfull, wself, wneigh, cot, act, direct, scaled, wgrad,
                 rx, xn, av, gr, send, recv, rs, rr, ss, sr):
    y, z, x, feat = place()
    node = node_of(y, z, x)
    HALF = TPN // 2
    SPAN = ROWS // 2

    def xof(k):
        return lax.rem(x + k + 2 * NX, NX)

    def xdev(s):
        return (node_of(y, z, xof(s)), feat)

    meet([xdev(1), xdev(-1), (node, across(feat)), (node, sibling(feat))])

    def cut(s):
        return pl.ds(side(s) * HALF, HALF)

    def hop(s, step):
        i = (side(s), step)
        if step == 0:
            src, dst = part.at[xof(2 * s), cut(s)], rx.at[side(s), 1]
        elif step == 1:
            src, dst = part.at[xof(s), cut(-s)], rx.at[2 + side(s), 1]
        else:
            src, dst = rx.at[side(s), 1], rx.at[side(s), 0]
        return remote(src, dst, rs.at[i], rr.at[i], xdev(s))

    for step in range(2):
        for s in BOTH:
            hop(s, step).start()

    off = pl.multiple_of(feat * FC, FC)

    def cols_of(k, which):
        return wfull[k, pl.ds(which * 256 + off, FC), :]

    perm = order()
    for k in range(4):
        for t in range(TPN):
            xn[k, :, t * TILE:(t + 1) * TILE] = dot(xfull[k, t], perm).astype(BF)
    for s in BOTH:
        hop(s, 0).wait_recv()
        rx[side(s), 1] += part[xof(s), cut(s)]
        hop(s, 2).start()
    pre = dot(cols_of(0, 0), xn[0])
    for k in range(1, 4):
        pre += dot(cols_of(k, 0), xn[k])
    for s in BOTH:
        hop(s, 1).wait_recv()
        hop(s, 2).wait_recv()

    def share(ref, sems, c):
        return exchange(ref.at[feat, c], lambda k: ref.at[k, c], feat, node, sems, send, recv)

    degrees, first = [], []
    for r in range(TPN):
        near, far = (0, 1) if r < HALF else (1, 0)
        q = r % HALF
        total = part[x, r] + rx[near, 0, q] + rx[2 + far, 1, q]
        degree = jnp.maximum(jnp.sum(total[FC:], axis=0, keepdims=True), 1.0)
        degrees.append(degree)
        av[feat, r // HALF, :, q * TILE:(q + 1) * TILE] = (total[:FC] / degree).astype(BF)
        if q == HALF - 1:
            first.append(share(av, 3 * (r // HALF), r // HALF))
    for step, _ in first:
        step()
    second = []
    for c in range(2):
        first[c][1]()
        span = slice(c * SPAN, (c + 1) * SPAN)
        own = pre[:, span]
        for k in range(4):
            own += dot(cols_of(k, 1), av[k, c])
        sig = jax.nn.sigmoid(own)
        grad = cot[:, span] * sig * (1.0 + own * (1.0 - sig))
        gr[feat, c] = grad.astype(BF)
        second.append(share(gr, 6 + 3 * c, c))
        act[:, span] = own * sig
    for step, _ in second:
        step()

    def shop(s, c, d, arriving=False):
        i = (side(s), c, d - 1)
        at = scaled.at[xof(-s * d if arriving else -s * (d - 1)), pl.ds(c * HALF, HALF)]
        return remote(at, at, ss.at[i], sr.at[i], xdev(s))

    for c in range(2):
        second[c][1]()
        sums = dot(wneigh[:, 0:FC], gr[0, c])
        for k in range(1, 4):
            sums += dot(wneigh[:, k * FC:(k + 1) * FC], gr[k, c])
        for q in range(HALF):
            r = c * HALF + q
            scaled[x, r] = (sums[:, q * TILE:(q + 1) * TILE] / degrees[r]).astype(BF)
        for s in BOTH:
            shop(s, c, 1).start()
    for c in range(2):
        straight = dot(wself[:, 0:FC], gr[0, c])
        for k in range(1, 4):
            straight += dot(wself[:, k * FC:(k + 1) * FC], gr[k, c])
        direct[:, c * SPAN:(c + 1) * SPAN] = straight
    for c in range(2):
        for s in BOTH:
            shop(s, c, 1, True).wait_recv()
            if c == side(s):
                shop(s, c, 2).start()
    for k in range(4):
        lanes = slice(k * FC, (k + 1) * FC)
        wgrad[0:FC, lanes] = nt(xn[feat, :, 0:SPAN], gr[k, 0]) + nt(xn[feat, :, SPAN:ROWS], gr[k, 1])
        wgrad[FC:2 * FC, lanes] = nt(av[feat, 0], gr[k, 0]) + nt(av[feat, 1], gr[k, 1])
    for s in BOTH:
        shop(s, side(s), 2, True).wait_recv()
        shop(s, side(s), 2).wait_send()
        for c in range(2):
            shop(s, c, 1).wait_send()
        for step in range(3):
            hop(s, step).wait_send()


def dense(part, xfull, wfull, wself, wneigh, cot):
    dma = pltpu.SemaphoreType.DMA
    return pl.pallas_call(
        dense_kernel,
        out_shape=(
            jax.ShapeDtypeStruct((FC, ROWS), F32),
            jax.ShapeDtypeStruct((FC, ROWS), F32),
            OUT((NX, TPN, FC, TILE), BF),
            OUT((2 * FC, 4 * FC), F32),
        ),
        in_specs=[VMEM] * 6,
        out_specs=(VMEM,) * 4,
        scratch_shapes=[
            pltpu.VMEM((4, 2, TPN // 2, FC + CNT, TILE), F32), pltpu.VMEM((4, FC, ROWS), BF),
            pltpu.VMEM((4, 2, FC, ROWS // 2), BF), pltpu.VMEM((4, 2, FC, ROWS // 2), BF),
            dma((12,)), dma((12,)), dma((2, 3)), dma((2, 3)), dma((2, 2, 2)), dma((2, 2, 2)),
        ],
        compiler_params=pltpu.CompilerParams(
            collective_id=1, has_side_effects=True, vmem_limit_bytes=24 * 2**20
        ),
        name="dense",
    )(part, xfull, wfull, wself, wneigh, cot)


def backward_kernel(slots, edges, source, out, acc):
    acc[...] = jnp.zeros_like(acc)
    count = slots[8, 0]

    def group(g, _):
        for u in range(UNROLL):
            row, col, planes = entry(slots, g, u, count, edges)
            block, tile = lax.shift_right_logical(row, 3), jnp.bitwise_and(row, 7)
            acc[col] += nt(source[block, tile], planes.astype(BF))
        return 0

    lax.fori_loop(0, (count + UNROLL - 1) // UNROLL, group, 0)
    for y in range(NY):
        for z in range(NZ):
            base = (y * NZ + z) * TPN
            out[y, z] = acc[base:base + TPN].astype(BF)


def backward(slots, edges, source):
    return pl.pallas_call(
        backward_kernel,
        out_shape=OUT((NY, NZ, TPN, FC, TILE), BF),
        in_specs=[SMEM, VMEM, VMEM],
        out_specs=VMEM,
        scratch_shapes=[pltpu.VMEM((NY * NZ * TPN, FC, TILE), F32)],
        compiler_params=pltpu.CompilerParams(vmem_limit_bytes=24 * 2**20),
        name="backward_sums",
    )(slots, edges, source)


def scatter_kernel(part, wgrad, out, wout, rz, ry, w1, w2, zs, zr, ys, yr, ws, wr):
    y, z, x, feat = place()
    oy = 1 - y
    HALF = TPN // 2

    def zof(k):
        return lax.rem(z + k + 2 * NZ, NZ)

    def yof(j):
        return y + j - 2 * j * y

    def zdev(s):
        return (node_of(y, zof(s), x), feat)

    plane = y * NX + x

    def pdev(k):
        p = lax.rem(plane + k, NY * NX)
        return (node_of(p // NX, z, lax.rem(p, NX)), feat)

    meet([zdev(k) for k in range(1, NZ)] + [pdev(k) for k in range(1, NY * NX)])
    ydev = (node_of(oy, z, x), feat)

    def starts(s, c, d):
        return d == (4 if c == side(s) else 3)

    def hop(s, j, c, d):
        i = (side(s), j, c, d - 1)
        src = rz.at[side(s), j, c, min(d, 3)]
        if starts(s, c, d):
            src = part.at[yof(j), zof(s * d), pl.ds(c * HALF, HALF)]
        return remote(src, rz.at[i], zs.at[i], zr.at[i], zdev(s))

    def yhop(c):
        return remote(rz.at[0, 1, c, 0], ry.at[c], ys.at[c], yr.at[c], ydev)

    def wcopy(phase, k):
        i = phase * 7 + k - 1
        if phase == 0:
            return remote(wgrad.at[pl.ds(pl.multiple_of(zof(k) * 16, 16), 16)], w1.at[k - 1], ws.at[i], wr.at[i], zdev(k))
        if phase == 1:
            return remote(w2.at[plane], w2.at[plane], ws.at[i], wr.at[i], pdev(k))
        rows = pl.ds(pl.multiple_of(z * 16, 16), 16)
        return remote(wout.at[rows], wout.at[rows], ws.at[i], wr.at[i], zdev(k))

    def wexpect(phase, k):
        i = phase * 7 + k - 1
        if phase == 0:
            dst = w1.at[k - 1]
        elif phase == 1:
            dst = w2.at[lax.rem(plane + NY * NX - k, NY * NX)]
        else:
            dst = wout.at[pl.ds(pl.multiple_of(zof(-k) * 16, 16), 16)]
        return remote(dst, dst, ws.at[i], wr.at[i], zdev(k))

    for j in (1, 0):
        for s in BOTH:
            hop(s, j, side(s), 4).start()
    for k in range(1, NZ):
        wcopy(0, k).start()
    for j in (1, 0):
        for s in BOTH:
            hop(s, j, 1 - side(s), 3).start()
    for d in (4, 3, 2):
        for j in (1, 0):
            for c in range(2):
                for s in BOTH:
                    if d == 4 and c != side(s):
                        continue
                    hop(s, j, c, d).wait_recv()
                    i = (side(s), j, c, d - 1)
                    term = part[yof(j), zof(s * (d - 1)), c * HALF:(c + 1) * HALF]
                    rz[i] = (rz[i].astype(F32) + term.astype(F32)).astype(BF)
                    hop(s, j, c, d - 1).start()
        if d == 4:
            for k in range(1, NZ):
                wexpect(0, k).wait_recv()
            acc = wgrad[pl.ds(pl.multiple_of(z * 16, 16), 16)]
            for k in range(1, NZ):
                acc += w1[k - 1]
            w2[plane] = acc
            for k in range(1, NY * NX):
                wcopy(1, k).start()
        if d == 3:
            for k in range(1, NY * NX):
                wexpect(1, k).wait_recv()
            acc = w2[0]
            for k in range(1, NY * NX):
                acc += w2[k]
            wout[pl.ds(pl.multiple_of(z * 16, 16), 16)] = acc
            for k in range(1, NZ):
                wcopy(2, k).start()

    def total(j, c):
        for s in BOTH:
            hop(s, j, c, 1).wait_recv()
        mine = part[yof(j), z, c * HALF:(c + 1) * HALF].astype(F32)
        return mine + rz[0, j, c, 0].astype(F32) + rz[1, j, c, 0].astype(F32)

    for c in range(2):
        rz[0, 1, c, 0] = total(1, c).astype(BF)
        yhop(c).start()
    for c in range(2):
        mine = total(0, c)
        yhop(c).wait_recv()
        out[c * HALF:(c + 1) * HALF] = mine + ry[c].astype(F32)
    for k in range(1, NZ):
        wexpect(2, k).wait_recv()
    for s in BOTH:
        for j in range(2):
            for c in range(2):
                for d in range(1, 5 if c == side(s) else 4):
                    hop(s, j, c, d).wait_send()
    for c in range(2):
        yhop(c).wait_send()
    for phase in range(3):
        for k in range(1, 8):
            wcopy(phase, k).wait_send()


def scatter(part, wgrad):
    dma = pltpu.SemaphoreType.DMA
    return pl.pallas_call(
        scatter_kernel,
        out_shape=(
            jax.ShapeDtypeStruct((TPN, FC, TILE), F32),
            jax.ShapeDtypeStruct((2 * FC, 4 * FC), F32),
        ),
        in_specs=[VMEM, VMEM],
        out_specs=(VMEM, VMEM),
        scratch_shapes=[
            pltpu.VMEM((2, 2, 2, 4, TPN // 2, FC, TILE), BF),
            pltpu.VMEM((2, TPN // 2, FC, TILE), BF),
            pltpu.VMEM((NZ - 1, 16, 256), F32),
            pltpu.VMEM((NY * NX, 16, 256), F32),
            dma((2, 2, 2, 4)), dma((2, 2, 2, 4)), dma((2,)), dma((2,)), dma((21,)), dma((21,)),
        ],
        compiler_params=pltpu.CompilerParams(
            collective_id=2, has_side_effects=True, vmem_limit_bytes=24 * 2**20
        ),
        name="scatter",
    )(part, wgrad)


def local(features, w_self, w_neigh, tile_rows, tile_cols, tile_count, edge_bits, cotangent):
    rows, cols = tile_rows.reshape(2, TILE), tile_cols.reshape(2, TILE)
    full, xfull, wfull, edges, slots = gather(features, w_self, w_neigh, rows, cols, tile_count, edge_bits)
    part = forward(slots, edges, full)
    act, direct, scaled, wgrad = dense(part, xfull, wfull, w_self, w_neigh, cotangent.T)
    part = backward(slots, edges, scaled)
    back, wsum = scatter(part, wgrad)
    back = back.reshape(TPN, FC, 8, TILE // 8).transpose(0, 3, 2, 1).reshape(ROWS, FC)
    return act.T, direct.T + back, wsum[:FC], wsum[FC:]


def solution(mesh):
    placed = (
        P("node", "feat"),
        P("feat", None),
        P("feat", None),
        P("node"),
        P("node"),
        P("node"),
        P("node", None, None),
        P("node", "feat"),
    )
    return jax.shard_map(
        local,
        mesh=mesh,
        in_specs=placed,
        out_specs=(P("node", "feat"), P("node", "feat"), P("feat", None), P("feat", None)),
        check_vma=False,
    )
```

time: 1360 us -> 125 us (0.09)
  waiting for transfers between devices: 1190 us -> 0 us
  Pallas kernels: 0 us -> 114 us
  matrix products: 60.6 us -> 0 us
  other arithmetic: 47.2 us -> 0.73 us
  local copies, waits for them, and re-layouts: 43.5 us -> 7.44 us
    psum x1 -> x0, waiting for transfers between devices: 606 us -> none  [local(): grad_self, grad_neigh = lax.psum((part_self, part_neigh), 'node')]
    reduce_scatter x2 -> x0, waiting for transfers between devices: 418 us -> none  [the longest x1 397 us: local(): lax.psum_scatter(accum.reshape(all_tiles * tile_size, feat_cols), 'node',...]
    all_gather x2 -> x0, waiting for transfers between devices: 169 us -> none  [the longest x1 144 us: local(): gathered = lax.all_gather(features, 'node', axis=0, tiled=True)]
    pallas_call x0 -> x5, Pallas kernels: none -> 114 us  [the longest x1 40.1 us: scatter(): pl.pallas_call(scatter_kernel, out_shape=(jax.ShapeDtypeStruct((TPN, FC,...]
    dot_general x10 -> x0, matrix products: 60.6 us -> none  [the longest x1 37.2 us: local(): contrib = jnp.einsum('tqp,tpf->tqf', mask_f32, source, precision=hi)]
    scatter-add x1 -> x0, other arithmetic: 39.4 us -> none  [local(): jnp.zeros((all_tiles, tile_size, feat_cols), jnp.float32).at[tile_cols]]
    reshape x3 -> x1, local copies, waits for them, and re-layouts: 20.4 us -> 0.18 us  [local(): back.reshape(TPN, FC, 8, TILE // 8).transpose(0, 3, 2, 1).reshape(ROWS, FC)]
  transfers between devices with their start and end apart: 5 -> 0, of which waited for: 5 -> 0; matrix products, arithmetic and copies ran while one was open for 1% -> 0% of each run, Pallas kernels for 0% -> 0%
where the time goes in v2:
time: 125 us; the launch traced here: 124 us
  Pallas kernels  114 us (91%)
  local copies, waits for them, and re-layouts  7.44 us (6%)
  between operations  1.37 us (1%)
    pallas_call x1, Pallas kernels, scatter(): pl.pallas_call(scatter_kernel, out_shape=(jax.ShapeDtypeStruct((TPN, FC,...  40.1 us
    pallas_call x1, Pallas kernels, gather(): pl.pallas_call(gather_kernel, out_shape=(OUT((NY, NZ, TPN, FC, TILE), BF)...  33.3 us
    pallas_call x1, Pallas kernels, dense(): pl.pallas_call(dense_kernel, out_shape=(jax.ShapeDtypeStruct((FC, ROWS),...  30.6 us
    unnamed x14, local copies, waits for them, and re-layouts  6.24 us
    pallas_call x1, Pallas kernels, backward(): pl.pallas_call(backward_kernel, out_shape=OUT((NY, NZ, TPN, FC, TILE), BF...  5.88 us
    pallas_call x1, Pallas kernels, forward(): pl.pallas_call(forward_kernel, out_shape=OUT((NX, TPN, FC + CNT, TILE), F...  4.34 us

profile of v2, /device:TPU:24, one launch (start us, length us, event | category | flops | bytes accessed | tf_op | source)
XLA Modules:
  0.0 123.7 jit_solution(5625326217045526205)
XLA Ops:
  1.3 1.1 copy.14.feats
  2.4 0.0 copy-start
  2.4 1.6 %copy-done = s32[256,16,128]{2,1,0:T(8,128)S(1)} copy-done((s32[256,16,128]{2,1,0:T(8,128)S(1)}, s32[256,16,128]{2,1,0:T(8,128)}, u32[]{:S(2)}) %copy-start) | copy-done | bytes 2097176
  4.0 0.0 copy-start.2
  4.0 0.8 copy-done.2
  4.7 0.0 copy-start.3
  4.7 0.8 copy-done.3
  5.5 0.0 copy-start.4
  5.5 0.7 copy-done.4
  6.1 0.0 copy-start.5
  6.2 0.7 copy-done.5
  6.8 33.3 %gather.1 = (bf16[2,8,8,64,128]{4,3,2,1,0:T(8,128)(2,1)S(1)}, bf16[4,8,64,128]{3,2,1,0:T(8,128)(2,1)S(1)}, bf16[4,512,64]{2,1,0:T(8,128)(2,1)S(1)}, s16[4,256,16,128]{3,2,1,0:T(8,128)(2,1)S(1)}, s32[16,128]{1,0:T(8,128)S(1)}) custom-call(bf16[1024,64]{1,0:T(8,128)(2,1)S(1)} %copy.14.feats, bf16[64,256]{1,0:T(8,128)(2,1)S(1)} %copy-done.2, ...), custom_call_target="tpu_custom_call" | custom-call | tf_op jit(solution)/shard_map/gather/pallas_call | solution.py:296
  40.1 0.0 copy-start.1
  40.1 4.3 %forward_sums.1.part = f32[4,8,72,128]{3,2,1,0:T(8,128)S(1)} custom-call(s32[16,128]{1,0:T(8,128)S(1)} %get-tuple-element.15.slots, s16[4,256,16,128]{3,2,1,0:T(8,128)(2,1)S(1)} %get-tuple-element.16.edges, bf16[2,8,8,64,128]{4,3,2,1,0:T(8,128)(2,1)S(1)} %get-tuple-element.17.full), custom_call_target="tpu_custom_call" | custom-call | tf_op jit(solution)/shard_map/forward_sums/pallas_call | solution.py:352
  44.5 0.0 copy-done.1
  44.5 30.6 %dense.1 = (f32[64,1024]{1,0:T(8,128)S(1)}, f32[64,1024]{1,0:T(8,128)S(1)}, bf16[4,8,64,128]{3,2,1,0:T(8,128)(2,1)S(1)}, f32[128,256]{1,0:T(8,128)S(1)}) custom-call(f32[4,8,72,128]{3,2,1,0:T(8,128)S(1)} %forward_sums.1.part, bf16[4,8,64,128]{3,2,1,0:T(8,128)(2,1)S(1)} %get-tuple-element.18.xfull, bf16[4,512,64]{2,1,0:T(8,128)(2,1)S(1)} %get-tuple-element.19.wfull, ...), custom_call_target="tpu_custom_call" | custom-call | tf_op jit(solution)/shard_map/dense/pallas_call | solution.py:484
  75.1 5.9 %backward_sums.1.part = bf16[2,8,8,64,128]{4,3,2,1,0:T(8,128)(2,1)S(1)} custom-call(s32[16,128]{1,0:T(8,128)S(1)} %get-tuple-element.15.slots, s16[4,256,16,128]{3,2,1,0:T(8,128)(2,1)S(1)} %get-tuple-element.16.edges, bf16[4,8,64,128]{3,2,1,0:T(8,128)(2,1)S(1)} %get-tuple-element.22.source), custom_call_target="tpu_custom_call" | custom-call | tf_op jit(solution)/shard_map/backward_sums/pallas_call | solution.py:525
  81.0 40.1 %scatter.1 = (f32[8,64,128]{2,1,0:T(8,128)S(1)}, f32[128,256]{1,0:T(8,128)S(1)}) custom-call(bf16[2,8,8,64,128]{4,3,2,1,0:T(8,128)(2,1)S(1)} %backward_sums.1.part, f32[128,256]{1,0:T(8,128)S(1)} %get-tuple-element.23.wgrad), custom_call_target="tpu_custom_call" | custom-call | tf_op jit(solution)/shard_map/scatter/pallas_call | solution.py:658
  121.0 0.7 fusion
  121.7 0.2 copy.15
  121.9 0.2 copy.16
  122.1 0.2 copy.17
  122.3 0.7 bitcast_add_fusion
  123.0 0.7 copy.20
Async XLA Ops:
  2.4 1.6 %copy-start = (s32[256,16,128]{2,1,0:T(8,128)S(1)}, s32[256,16,128]{2,1,0:T(8,128)}, u32[]{:S(2)}) copy-start(s32[256,16,128]{2,1,0:T(8,128)} %words.1) | copy-start | bytes 6291460
  4.0 0.8 copy-start.2
  4.7 0.8 copy-start.3
  5.5 0.7 copy-start.4
  6.1 0.7 copy-start.5
  40.1 4.4 %copy-start.1 = (f32[1024,64]{0,1:T(8,128)S(1)}, f32[1024,64]{0,1:T(8,128)}, u32[]{:S(2)}) copy-start(f32[1024,64]{0,1:T(8,128)} %param.15) | copy-start | bytes 786436

commit v3 on v2

v3 whole, which is shorter than its diff:
```python
import jax
import jax.numpy as jnp
from jax import lax
from jax.experimental import pallas as pl
from jax.experimental.pallas import tpu as pltpu
from jax.sharding import PartitionSpec as P

MESH = pl.DeviceIdType.MESH
BF = jnp.bfloat16
F32 = jnp.float32
NY, NZ, NX = 2, 8, 4
TPN = 8
FC = 64
TILE = 128
ROWS = TPN * TILE
SLOTS = 256
WORDS = 16
CNT = 16
BOTH = (1, -1)
UNROLL = 8
HBM = pl.BlockSpec(memory_space=pltpu.HBM)
VMEM = pl.BlockSpec(memory_space=pltpu.VMEM)
SMEM = pl.BlockSpec(memory_space=pltpu.SMEM)
OUT = pltpu.VMEM


def place():
    node, feat = lax.axis_index("node"), lax.axis_index("feat")
    return node // (NZ * NX), lax.rem(node // NX, NZ), lax.rem(node, NX), feat


def side(s):
    return 0 if s > 0 else 1


def node_of(y, z, x):
    return (y * NZ + z) * NX + x


def across(feat):
    return lax.rem(feat + 2, 4)


def sibling(feat):
    return feat + 1 - 2 * lax.rem(feat, 2)


def meet(peers):
    barrier = pltpu.get_barrier_semaphore()
    for peer in peers:
        pl.semaphore_signal(barrier, inc=1, device_id=peer, device_id_type=MESH)
    pl.semaphore_wait(barrier, len(peers))


def remote(src, dst, send, recv, peer):
    return pltpu.make_async_remote_copy(
        src_ref=src, dst_ref=dst, send_sem=send, recv_sem=recv, device_id=peer, device_id_type=MESH
    )


def exchange(mine, slot, feat, node, sems, send, recv):
    one, two = (node, across(feat)), (node, sibling(feat))
    far, near = across(feat), sibling(feat)
    diag = across(near)
    a = remote(mine, slot(feat), send.at[sems], recv.at[sems], one)
    b = remote(mine, slot(feat), send.at[sems + 1], recv.at[sems + 1], two)
    c = remote(slot(far), slot(far), send.at[sems + 2], recv.at[sems + 2], two)
    a.start()
    b.start()

    def step():
        remote(slot(far), slot(far), send.at[sems], recv.at[sems], one).wait_recv()
        c.start()

    def finish():
        remote(slot(near), slot(near), send.at[sems + 1], recv.at[sems + 1], two).wait_recv()
        remote(slot(diag), slot(diag), send.at[sems + 2], recv.at[sems + 2], two).wait_recv()
        a.wait_send()
        b.wait_send()
        c.wait_send()

    return step, finish


def dot(a, b):
    return jnp.dot(a, b, preferred_element_type=F32)


def nt(a, b):
    return lax.dot_general(a, b, (((1,), (1,)), ((), ())), preferred_element_type=F32)


def iota(shape, dim):
    return lax.broadcasted_iota(jnp.int32, shape, dim)


def order():
    old = iota((TILE, TILE), 1)
    new = jnp.bitwise_and(old, 7) * WORDS + lax.shift_right_logical(old, 3)
    return (iota((TILE, TILE), 0) == new).astype(F32).astype(BF)


ORDER = (
    "s0", "s1", "s2", "s3", "z21", "y", "z01", "e0", "z11", "e1", "z22", "z02", "c",
    "l0", "l1", "l2", "e2", "z12", "l3", "l4", "x", "z23", "e3", "l5", "z03", "h0",
    "l6", "z13", "l7", "i", "z24", "h1", "z04", "z14",
)


def gather_kernel(feats, wself, wneigh, rows, cols, count, words, full, xfull, wfull, edges, listed,
                  raw, ids, codes, marks,
                  zs, zr, es, er, bs, br, cs, cr, ys, yr, fs, fr, ls):
    y, z, x, feat = place()
    node = node_of(y, z, x)
    oy = 1 - y
    HALF = TPN // 2

    def zof(k):
        return lax.rem(z + k + 2 * NZ, NZ)

    def xof(k):
        return lax.rem(x + k + 2 * NX, NX)

    def zdev(s):
        return (node_of(y, zof(s), x), feat)

    def xdev(s):
        return (node_of(y, z, xof(s)), feat)

    ydev = (node_of(oy, z, x), feat)
    beside = (node, sibling(feat))
    peers = [zdev(1), zdev(-1), xdev(1), xdev(-1), xdev(2), ydev, (node, across(feat)), beside]
    barrier = pltpu.get_barrier_semaphore()
    for peer in peers:
        pl.semaphore_signal(barrier, inc=1, device_id=peer, device_id_type=MESH)

    half = lax.rem(feat, 2) * (SLOTS // 2)
    other = SLOTS // 2 - half
    PART = SLOTS // 8

    def load(c):
        base = half + c * PART if c < 4 else other
        span = pl.ds(base, PART if c < 4 else SLOTS // 2)
        return pltpu.make_async_copy(words.at[span], raw.at[span], ls.at[c])

    small = [
        pltpu.make_async_copy(a, b, ls.at[5 + i])
        for i, (a, b) in enumerate((
            (feats, xfull.at[feat]), (wself, wfull.at[feat, 0]), (wneigh, wfull.at[feat, 1]),
            (rows, ids.at[0]), (cols, ids.at[1]),
        ))
    ]
    small[0].start()
    for c in range(5):
        load(c).start()
    for copy in small[1:]:
        copy.start()
    perm = order()
    small[0].wait()
    for t in range(TPN):
        full[y, z, t] = nt(xfull[feat, :, t * TILE:(t + 1) * TILE], perm).astype(BF)
    for i in range(4):
        load(i).wait()
        span = pl.ds(half + i * PART, PART)
        edges[x, span] = raw[span].astype(jnp.int16)
    for copy in small[3:]:
        copy.wait()
    at = iota((2, TILE), 0) * TILE + iota((2, TILE), 1)
    codes[...] = jnp.full_like(codes, -1)
    codes[0:2] = jnp.where(at < count[0], ids[0] * 65536 + ids[1], -1)
    marks[x] = codes[...]
    pl.semaphore_wait(barrier, len(peers))

    def block(u, zr, d, s):
        base = (0, 0, HALF)[u] + (side(s) * (HALF // 2) if d == 4 else 0)
        return full.at[oy if u == 1 else y, zof(zr), pl.ds(base, HALF // 2 if d == 4 else HALF)]

    def zhop(s, u, d, arriving=False):
        i = (side(s), u, d - 1)
        at = block(u, -s * d if arriving else -s * (d - 1), d, s)
        return remote(at, at, zs.at[i], zr.at[i], zdev(s))

    def yhop(s, d, arriving=False):
        i = d if d < 1 else 1 + side(s) * 4 + d - 1
        i = 9 if d < 0 else i
        who = oy if arriving else y
        base = 0 if d < 0 else HALF
        base = base + (side(s) * (HALF // 2) if d == 4 else 0)
        at = full.at[who, zof(-s * max(d, 0)), pl.ds(base, HALF // 2 if d == 4 else HALF)]
        return remote(at, at, ys.at[i], yr.at[i], ydev)

    def ehop(s, c, d, arriving=False):
        i = (side(s), c, d - 1)
        at = edges.at[xof(-s * d if arriving else -s * (d - 1)), pl.ds(half + c * PART, PART)]
        return remote(at, at, es.at[i], er.at[i], xdev(s))

    def ehand(s, c, d, arriving=False):
        i = (side(s), c, d - 1)
        at = edges.at[xof(-s * d), pl.ds((other if arriving else half) + c * PART, PART)]
        return remote(at, at, bs.at[i], br.at[i], beside)

    def nth(s, i):
        return i if s > 0 else (i + 2) % 4

    def chop(k, arriving=False):
        at = marks.at[xof(-k) if arriving else x]
        return remote(codes if not arriving else at, at, cs.at[k - 1], cr.at[k - 1], xdev(k))

    yhop(1, -1).start()
    for s in BOTH:
        zhop(s, 2, 1).start()
        zhop(s, 0, 1).start()
    for k in range(1, NX):
        chop(k).start()
    yhop(1, 0).start()
    xstep, xfinish = exchange(feats, lambda k: xfull.at[k], feat, node, 0, fs, fr)
    wstep, wfinish = exchange(wself, lambda k: wfull.at[k, 0], feat, node, 3, fs, fr)
    vstep, vfinish = exchange(wneigh, lambda k: wfull.at[k, 1], feat, node, 6, fs, fr)
    small[1].wait()
    small[2].wait()

    def zpass(u, d):
        for s in BOTH:
            zhop(s, u, d, True).wait_recv()
            if d < 4:
                zhop(s, u, d + 1).start()
            if u == 2:
                yhop(s, d).start()

    def eround(i):
        for s in BOTH:
            c = nth(s, i)
            ehop(s, c, 1, True).wait_recv()
            if i < 2:
                ehop(s, c, 2).start()
            ehand(s, c, 1).start()

    def efar(i):
        for s in BOTH:
            c = nth(s, i)
            ehop(s, c, 2, True).wait_recv()
            ehand(s, c, 2).start()

    def efirst(i):
        for s in BOTH:
            ehop(s, nth(s, i), 1).start()

    def ycross():
        yhop(1, -1, True).wait_recv()
        for s in BOTH:
            zhop(s, 1, 1).start()

    def passon():
        for step in (xstep, wstep, vstep):
            step()

    state = {}

    def prepare():
        load(4).wait()
        span = pl.ds(other, SLOTS // 2)
        edges[x, span] = raw[span].astype(jnp.int16)
        for k in range(1, NX):
            chop(k, True).wait_recv()
        code = jnp.concatenate([marks[b, 0:2] for b in range(NX)], axis=0)
        col = jnp.bitwise_and(code, 511)
        mine = jnp.where(
            jnp.logical_and(code >= 0, jnp.bitwise_and(lax.shift_right_logical(col, 3), 3) == x), 1.0, 0.0
        )
        slot = iota((8, TILE), 0) * TILE + iota((8, TILE), 1)
        row = lax.shift_right_logical(slot, 8) * TPN + jnp.bitwise_and(lax.shift_right_arithmetic(code, 16), 7)
        near = lax.shift_left(lax.shift_right_logical(col, 5), 3) + jnp.bitwise_and(col, 7)
        upto = jnp.where(iota((TILE, TILE), 0) <= iota((TILE, TILE), 1), 1.0, 0.0).astype(BF)
        prefix = dot(mine.astype(BF), upto)
        pos = jnp.where(mine > 0.0, prefix - 1.0, -1.0e6)
        base = jnp.zeros((1, 1), F32)
        shifted = []
        for r in range(8):
            shifted.append(pos[r:r + 1] + base)
            base = base + prefix[r:r + 1, TILE - 1:TILE]
        pos = jnp.concatenate(shifted + [jnp.zeros((TILE - 8, TILE), F32)], axis=0).T
        wide = iota((TILE, 8 * TILE), 1).astype(F32)
        picked = jnp.zeros((8, 8 * TILE), F32)
        fields = (jnp.bitwise_and(slot, 255), lax.shift_right_logical(slot, 8), row, near)
        state.update(pos=pos, base=base, wide=wide, picked=picked, fields=fields)

    def pick(r):
        pos, wide, fields = state["pos"], state["wide"], state["fields"]
        hot = jnp.where(pos[:, r:r + 1] == wide, 1.0, 0.0).astype(BF)
        stack = jnp.concatenate([f[r:r + 1].astype(F32) for f in fields] + [jnp.zeros((4, TILE), F32)], axis=0)
        state["picked"] += dot(stack.astype(BF), hot)

    def enlist():
        picked, base = state["picked"], state["base"]
        items = (picked[0:1] + 256.0 * picked[1:2] + 1024.0 * picked[2:3] + 32768.0 * picked[3:4]).astype(jnp.int32)
        for r in range(8):
            listed[r:r + 1] = items[:, r * TILE:(r + 1) * TILE]
        listed[8:16] = jnp.broadcast_to(base, (8, TILE)).astype(jnp.int32)

    steps = {"z": zpass, "e": eround, "h": efar, "s": efirst, "y": ycross, "x": passon, "c": prepare, "l": pick, "i": enlist}
    for step in ORDER:
        steps[step[0]](*(int(digit) for digit in step[1:]))
    for s in BOTH:
        for i in range(4):
            c = nth(s, i)
            for d in (1, 2) if i < 2 else (1,):
                ehand(s, c, d, True).wait_recv()
                ehand(s, c, d).wait_send()
                ehop(s, c, d).wait_send()
        for d in range(1, 5):
            for u in range(3):
                zhop(s, u, d).wait_send()
            yhop(s, d, True).wait_recv()
            yhop(s, d).wait_send()
    yhop(1, 0, True).wait_recv()
    yhop(1, 0).wait_send()
    yhop(1, -1).wait_send()
    for k in range(1, NX):
        chop(k).wait_send()
    xfinish()
    wfinish()
    vfinish()


def gather(feats, wself, wneigh, rows, cols, count, words):
    dma = pltpu.SemaphoreType.DMA
    return pl.pallas_call(
        gather_kernel,
        out_shape=(
            OUT((NY, NZ, TPN, FC, TILE), BF),
            OUT((4, FC, ROWS), BF),
            OUT((4, 2, FC, 4 * FC), BF),
            OUT((NX, *words.shape), jnp.int16),
            jax.ShapeDtypeStruct((16, TILE), jnp.int32),
        ),
        in_specs=[HBM] * 5 + [SMEM, HBM],
        out_specs=(VMEM,) * 5,
        scratch_shapes=[
            pltpu.VMEM(words.shape, jnp.int32), pltpu.VMEM((2, 2, TILE), jnp.int32),
            pltpu.VMEM((8, TILE), jnp.int32), pltpu.VMEM((NX, 8, TILE), jnp.int32),
            dma((2, 3, 4)), dma((2, 3, 4)), dma((2, 4, 2)), dma((2, 4, 2)), dma((2, 4, 2)), dma((2, 4, 2)),
            dma((3,)), dma((3,)), dma((10,)), dma((10,)), dma((9,)), dma((9,)), dma((10,)),
        ],
        compiler_params=pltpu.CompilerParams(
            collective_id=0, has_side_effects=True, vmem_limit_bytes=24 * 2**20
        ),
        name="gather",
    )(feats, wself, wneigh, rows, cols, count, words)


def planes_of(words):
    one, zero = jnp.ones(words.shape, BF), jnp.zeros(words.shape, BF)
    return jnp.concatenate(
        [jnp.where(jnp.bitwise_and(words, jnp.int16(1 << b)) != 0, one, zero) for b in range(8)], axis=0
    )


def entry(slots, group, u, count, edges):
    item = slots[lax.shift_right_logical(group, 4), jnp.bitwise_and(group, 15) * UNROLL + u]
    words = edges[jnp.bitwise_and(lax.shift_right_logical(item, 8), 3), jnp.bitwise_and(item, 255)]
    planes = planes_of(jnp.where(group * UNROLL + u < count, words, jnp.zeros_like(words)))
    return jnp.bitwise_and(lax.shift_right_logical(item, 10), 31), lax.shift_right_logical(item, 15), planes


def forward_kernel(slots, edges, full, acc):
    acc[...] = jnp.zeros_like(acc)
    count = slots[8, 0]
    ones = jnp.ones((CNT, TILE), BF)

    def group(g, _):
        for u in range(UNROLL):
            row, col, planes = entry(slots, g, u, count, edges)
            near, t = lax.shift_right_logical(col, 3), jnp.bitwise_and(col, 7)
            block, tile = lax.shift_right_logical(row, 3), jnp.bitwise_and(row, 7)
            source = full[lax.shift_right_logical(near, 3), jnp.bitwise_and(near, 7), t]
            acc[block, tile] += dot(jnp.concatenate([source, ones], axis=0), planes)
        return 0

    lax.fori_loop(0, (count + UNROLL - 1) // UNROLL, group, 0)


def forward(slots, edges, full):
    return pl.pallas_call(
        forward_kernel,
        out_shape=OUT((NX, TPN, FC + CNT, TILE), F32),
        in_specs=[SMEM, VMEM, VMEM],
        out_specs=VMEM,
        compiler_params=pltpu.CompilerParams(vmem_limit_bytes=24 * 2**20),
        name="forward_sums",
    )(slots, edges, full)


def dense_kernel(part, xfull, wfull, wself, wneigh, cot, act, direct, scaled, wgrad,
                 pq, pm, rq, rm, av, gr, send, recv, rs, rr, ss, sr):
    y, z, x, feat = place()
    node = node_of(y, z, x)
    HALF = TPN // 2
    SPAN = ROWS // 2

    def xof(k):
        return lax.rem(x + k + 2 * NX, NX)

    def xdev(s):
        return (node_of(y, z, xof(s)), feat)

    peers = [xdev(1), xdev(-1), xdev(2), (node, across(feat)), (node, sibling(feat))]
    barrier = pltpu.get_barrier_semaphore()
    for peer in peers:
        pl.semaphore_signal(barrier, inc=1, device_id=peer, device_id_type=MESH)

    def pack(c, k):
        block = xof(k)
        for q in range(HALF):
            r = c * HALF + q
            sums = part[block, r, 0:FC]
            most = jnp.maximum(jnp.max(jnp.abs(sums), axis=0, keepdims=True), 1e-30)
            pq[c, k - 1, q] = jnp.round(sums * (32766.0 / most)).astype(jnp.int32).astype(jnp.int16)
            pm[c, k - 1, q:q + 1] = most * (1.0 / 32766.0)
            pm[c, k - 1, HALF + q:HALF + q + 1] = part[block, r, FC:FC + 1]

    def hop(c, k, what):
        i = (c, k - 1, what)
        src, dst = ((pq, rq), (pm, rm))[what]
        return remote(src.at[c, k - 1], dst.at[c, k - 1], rs.at[i], rr.at[i], xdev(k))

    ORDER = (2, 1, 3)
    for k in ORDER:
        pack(0, k)
    pl.semaphore_wait(barrier, len(peers))
    for c in range(2):
        for k in ORDER:
            if c == 1:
                pack(1, k)
            hop(c, k, 1).start()
            hop(c, k, 0).start()

    choose = (iota((FC, 4 * FC), 1) == iota((FC, 4 * FC), 0) + feat * FC).astype(F32).astype(BF)

    def cols_of(k, which):
        return nt(choose, wfull[k, which]).astype(BF)

    pre = dot(cols_of(0, 0), xfull[0])
    for k in range(1, 4):
        pre += dot(cols_of(k, 0), xfull[k])
    neigh = [cols_of(k, 1) for k in range(4)]

    def share(ref, sems, c):
        return exchange(ref.at[feat, c], lambda k: ref.at[k, c], feat, node, sems, send, recv)

    degrees, first = [], []
    for c in range(2):
        for k in ORDER:
            for what in (1, 0):
                hop(c, k, what).wait_recv()
        for q in range(HALF):
            r = c * HALF + q
            total = part[x, r, 0:FC]
            degree = part[x, r, FC:FC + 1]
            for k in range(3):
                total += rq[c, k, q].astype(jnp.int32).astype(F32) * rm[c, k, q:q + 1]
                degree += rm[c, k, HALF + q:HALF + q + 1]
            degree = jnp.maximum(degree, 1.0)
            degrees.append(degree)
            av[feat, c, :, q * TILE:(q + 1) * TILE] = (total / degree).astype(BF)
        first.append(share(av, 3 * c, c))
    for step, _ in first:
        step()
    second = []
    for c in range(2):
        first[c][1]()
        span = slice(c * SPAN, (c + 1) * SPAN)
        own = pre[:, span]
        for k in range(4):
            own += dot(neigh[k], av[k, c])
        sig = jax.nn.sigmoid(own)
        grad = cot[:, span] * sig * (1.0 + own * (1.0 - sig))
        gr[feat, c] = grad.astype(BF)
        second.append(share(gr, 6 + 3 * c, c))
        act[:, span] = own * sig
    for step, _ in second:
        step()

    def shop(s, c, d, arriving=False):
        i = (side(s), c, d - 1)
        at = scaled.at[xof(-s * d if arriving else -s * (d - 1)), pl.ds(c * HALF, HALF)]
        return remote(at, at, ss.at[i], sr.at[i], xdev(s))

    for c in range(2):
        second[c][1]()
        sums = dot(wneigh[:, 0:FC], gr[0, c])
        for k in range(1, 4):
            sums += dot(wneigh[:, k * FC:(k + 1) * FC], gr[k, c])
        for q in range(HALF):
            r = c * HALF + q
            scaled[x, r] = (sums[:, q * TILE:(q + 1) * TILE] / degrees[r]).astype(BF)
        for s in BOTH:
            shop(s, c, 1).start()
    for c in range(2):
        straight = dot(wself[:, 0:FC], gr[0, c])
        for k in range(1, 4):
            straight += dot(wself[:, k * FC:(k + 1) * FC], gr[k, c])
        direct[:, c * SPAN:(c + 1) * SPAN] = straight
    for c in range(2):
        for s in BOTH:
            shop(s, c, 1, True).wait_recv()
            if c == side(s):
                shop(s, c, 2).start()
    for k in range(4):
        lanes = slice(k * FC, (k + 1) * FC)
        wgrad[0:FC, lanes] = nt(xfull[feat, :, 0:SPAN], gr[k, 0]) + nt(xfull[feat, :, SPAN:ROWS], gr[k, 1])
        wgrad[FC:2 * FC, lanes] = nt(av[feat, 0], gr[k, 0]) + nt(av[feat, 1], gr[k, 1])
    for s in BOTH:
        shop(s, side(s), 2, True).wait_recv()
        shop(s, side(s), 2).wait_send()
        for c in range(2):
            shop(s, c, 1).wait_send()
    for c in range(2):
        for k in ORDER:
            for what in range(2):
                hop(c, k, what).wait_send()


def dense(part, xfull, wfull, wself, wneigh, cot):
    dma = pltpu.SemaphoreType.DMA
    return pl.pallas_call(
        dense_kernel,
        out_shape=(
            jax.ShapeDtypeStruct((FC, ROWS), F32),
            OUT((FC, ROWS), F32),
            OUT((NX, TPN, FC, TILE), BF),
            OUT((2 * FC, 4 * FC), F32),
        ),
        in_specs=[VMEM] * 6,
        out_specs=(VMEM,) * 4,
        scratch_shapes=[
            pltpu.VMEM((2, 3, TPN // 2, FC, TILE), jnp.int16), pltpu.VMEM((2, 3, 8, TILE), F32),
            pltpu.VMEM((2, 3, TPN // 2, FC, TILE), jnp.int16), pltpu.VMEM((2, 3, 8, TILE), F32),
            pltpu.VMEM((4, 2, FC, ROWS // 2), BF), pltpu.VMEM((4, 2, FC, ROWS // 2), BF),
            dma((12,)), dma((12,)), dma((2, 3, 2)), dma((2, 3, 2)), dma((2, 2, 2)), dma((2, 2, 2)),
        ],
        compiler_params=pltpu.CompilerParams(
            collective_id=1, has_side_effects=True, vmem_limit_bytes=24 * 2**20
        ),
        name="dense",
    )(part, xfull, wfull, wself, wneigh, cot)


def backward_kernel(slots, edges, source, act, out, acted, acc):
    acted[...] = act[...]
    acc[...] = jnp.zeros_like(acc)
    count = slots[8, 0]

    def group(g, _):
        for u in range(UNROLL):
            row, col, planes = entry(slots, g, u, count, edges)
            block, tile = lax.shift_right_logical(row, 3), jnp.bitwise_and(row, 7)
            acc[col] += nt(source[block, tile], planes)
        return 0

    lax.fori_loop(0, (count + UNROLL - 1) // UNROLL, group, 0)
    for y in range(NY):
        for z in range(NZ):
            base = (y * NZ + z) * TPN
            out[y, z] = acc[base:base + TPN].astype(BF)


def backward(slots, edges, source, act):
    return pl.pallas_call(
        backward_kernel,
        out_shape=(OUT((NY, NZ, TPN, FC, TILE), BF), jax.ShapeDtypeStruct((FC, ROWS), F32)),
        in_specs=[SMEM, VMEM, VMEM, VMEM],
        out_specs=(VMEM, VMEM),
        scratch_shapes=[pltpu.VMEM((NY * NZ * TPN, FC, TILE), F32)],
        compiler_params=pltpu.CompilerParams(vmem_limit_bytes=24 * 2**20),
        name="backward_sums",
    )(slots, edges, source, act)


def scatter_kernel(part, wgrad, direct, out, wout, rz, ry, rl, w1, w2, zs, zr, ys, yr, ws, wr):
    y, z, x, feat = place()
    oy = 1 - y
    HALF = TPN // 2
    CUT = HALF // 2

    def zof(k):
        return lax.rem(z + k + 2 * NZ, NZ)

    def zdev(s):
        return (node_of(y, zof(s), x), feat)

    plane = y * NX + x

    def pdev(k):
        p = lax.rem(plane + k, NY * NX)
        return (node_of(p // NX, z, lax.rem(p, NX)), feat)

    meet([zdev(k) for k in range(1, NZ)] + [pdev(k) for k in range(1, NY * NX)])
    ydev = (node_of(oy, z, x), feat)

    def term(u, k):
        if u == 2:
            return ry.at[(k + NZ) % NZ]
        return part.at[oy if u == 1 else y, zof(k), pl.ds(0, HALF)]

    def hop(s, u, d):
        i = (side(s), u, d - 1)
        if d == 4:
            cut = pl.ds(side(s) * CUT, CUT)
            return remote(term(u, 4).at[cut], rz.at[i].at[cut], zs.at[i], zr.at[i], zdev(s))
        return remote(rz.at[side(s), u, d], rz.at[i], zs.at[i], zr.at[i], zdev(s))

    def yhop(k):
        return remote(part.at[oy, zof(k), pl.ds(HALF, HALF)], ry.at[(k + NZ) % NZ],
                      ys.at[(k + NZ) % NZ], yr.at[(k + NZ) % NZ], ydev)

    def join(k):
        yhop(k).wait_recv()
        at = (k + NZ) % NZ
        ry[at] = (ry[at].astype(F32) + part[y, zof(k), HALF:TPN].astype(F32)).astype(BF)

    last = remote(rz.at[0, 1, 0], rl, ys.at[NZ], yr.at[NZ], ydev)

    def wcopy(phase, k):
        i = phase * 7 + k - 1
        if phase == 0:
            return remote(wgrad.at[pl.ds(pl.multiple_of(zof(k) * 16, 16), 16)], w1.at[k - 1], ws.at[i], wr.at[i], zdev(k))
        if phase == 1:
            return remote(w2.at[plane], w2.at[plane], ws.at[i], wr.at[i], pdev(k))
        rows = pl.ds(pl.multiple_of(z * 16, 16), 16)
        return remote(wout.at[rows], wout.at[rows], ws.at[i], wr.at[i], zdev(k))

    def wexpect(phase, k):
        i = phase * 7 + k - 1
        if phase == 0:
            dst = w1.at[k - 1]
        elif phase == 1:
            dst = w2.at[lax.rem(plane + NY * NX - k, NY * NX)]
        else:
            dst = wout.at[pl.ds(pl.multiple_of(zof(-k) * 16, 16), 16)]
        return remote(dst, dst, ws.at[i], wr.at[i], zdev(k))

    for k in (4, 3, -3):
        yhop(k).start()
    for u in (1, 0):
        for s in BOTH:
            hop(s, u, 4).start()
    for k in (2, -2, 1, -1, 0):
        yhop(k).start()
    for k in range(1, NZ):
        wcopy(0, k).start()
    join(4)
    for s in BOTH:
        hop(s, 2, 4).start()
    for d in (4, 3, 2):
        for u in (1, 0, 2):
            if u == 2:
                join(d - 1)
                join(1 - d)
            for s in BOTH:
                hop(s, u, d).wait_recv()
                i = (side(s), u, d - 1)
                more = term(u, s * (d - 1))
                if d == 4:
                    a, b = pl.ds(side(s) * CUT, CUT), pl.ds((1 - side(s)) * CUT, CUT)
                    rz[(*i, a)] = (rz[(*i, a)].astype(F32) + more[a].astype(F32)).astype(BF)
                    rz[(*i, b)] = more[b]
                else:
                    rz[i] = (rz[i].astype(F32) + more[...].astype(F32)).astype(BF)
                hop(s, u, d - 1).start()
        if d == 4:
            for k in range(1, NZ):
                wexpect(0, k).wait_recv()
            acc = wgrad[pl.ds(pl.multiple_of(z * 16, 16), 16)]
            for k in range(1, NZ):
                acc += w1[k - 1]
            w2[plane] = acc
            for k in range(1, NY * NX):
                wcopy(1, k).start()
        if d == 3:
            for k in range(1, NY * NX):
                wexpect(1, k).wait_recv()
            acc = w2[0]
            for k in range(1, NY * NX):
                acc += w2[k]
            wout[pl.ds(pl.multiple_of(z * 16, 16), 16)] = acc
            for k in range(1, NZ):
                wcopy(2, k).start()

    def total(u):
        for s in BOTH:
            hop(s, u, 1).wait_recv()
        return term(u, 0)[...].astype(F32) + rz[0, u, 0].astype(F32) + rz[1, u, 0].astype(F32)

    perm = order().astype(F32)

    def finish(t, sums):
        back = jnp.dot(sums, perm, preferred_element_type=F32, precision=lax.Precision.HIGHEST)
        lanes = slice(t * TILE, (t + 1) * TILE)
        out[:, lanes] = direct[:, lanes] + back

    rz[0, 1, 0] = total(1).astype(BF)
    last.start()
    join(0)
    sums = total(2)
    for t in range(HALF):
        finish(HALF + t, sums[t])
    sums = total(0)
    last.wait_recv()
    sums += rl[...].astype(F32)
    for t in range(HALF):
        finish(t, sums[t])
    for k in range(1, NZ):
        wexpect(2, k).wait_recv()
    for s in BOTH:
        for u in range(3):
            for d in range(1, 5):
                hop(s, u, d).wait_send()
    for k in range(NZ):
        yhop(k).wait_send()
    last.wait_send()
    for phase in range(3):
        for k in range(1, 8):
            wcopy(phase, k).wait_send()


def scatter(part, wgrad, direct):
    dma = pltpu.SemaphoreType.DMA
    return pl.pallas_call(
        scatter_kernel,
        out_shape=(
            jax.ShapeDtypeStruct((FC, ROWS), F32),
            jax.ShapeDtypeStruct((2 * FC, 4 * FC), F32),
        ),
        in_specs=[VMEM, VMEM, VMEM],
        out_specs=(VMEM, VMEM),
        scratch_shapes=[
            pltpu.VMEM((2, 3, 4, TPN // 2, FC, TILE), BF),
            pltpu.VMEM((NZ, TPN // 2, FC, TILE), BF),
            pltpu.VMEM((TPN // 2, FC, TILE), BF),
            pltpu.VMEM((NZ - 1, 16, 256), F32),
            pltpu.VMEM((NY * NX, 16, 256), F32),
            dma((2, 3, 4)), dma((2, 3, 4)), dma((NZ + 1,)), dma((NZ + 1,)), dma((21,)), dma((21,)),
        ],
        compiler_params=pltpu.CompilerParams(
            collective_id=2, has_side_effects=True, vmem_limit_bytes=24 * 2**20
        ),
        name="scatter",
    )(part, wgrad, direct)


def local(features, w_self, w_neigh, tile_rows, tile_cols, tile_count, edge_bits, cotangent):
    rows, cols = tile_rows.reshape(2, TILE), tile_cols.reshape(2, TILE)
    given = [
        pltpu.with_memory_space_constraint(a, pltpu.HBM)
        for a in (features.T, w_self, w_neigh, rows, cols, edge_bits)
    ]
    full, xfull, wfull, edges, slots = gather(*given[:5], tile_count, given[5])
    part = forward(slots, edges, full)
    act, direct, scaled, wgrad = dense(part, xfull, wfull, w_self, w_neigh, cotangent.T)
    part, act = backward(slots, edges, scaled, act)
    grad, wsum = scatter(part, wgrad, direct)
    return act.T, grad.T, wsum[:FC], wsum[FC:]


def solution(mesh):
    placed = (
        P("node", "feat"),
        P("feat", None),
        P("feat", None),
        P("node"),
        P("node"),
        P("node"),
        P("node", None, None),
        P("node", "feat"),
    )
    return jax.shard_map(
        local,
        mesh=mesh,
        in_specs=placed,
        out_specs=(P("node", "feat"), P("node", "feat"), P("feat", None), P("feat", None)),
        check_vma=False,
    )
```

time: 125 us -> 105 us (0.84)
  Pallas kernels: 114 us -> 101 us
  local copies, waits for them, and re-layouts: 7.44 us -> 1.38 us
    pallas_call x2, Pallas kernels: 45.9 us -> 39.8 us  [the longest x1 33.2 us: scatter(): pl.pallas_call(scatter_kernel, out_shape=(jax.ShapeDtypeStruct((FC, ROWS)...]
    unnamed x14 -> x7, local copies, waits for them, and re-layouts: 6.24 us -> 0.72 us
    pallas_call x1, Pallas kernels: 30.6 us -> 26.5 us  [dense(): pl.pallas_call(dense_kernel, out_shape=(jax.ShapeDtypeStruct((FC, ROWS),...]
    pallas_call x1, Pallas kernels: 33.3 us -> 29.9 us  [gather(): pl.pallas_call(gather_kernel, out_shape=(OUT((NY, NZ, TPN, FC, TILE), BF)...]
where the time goes in v3:
time: 105 us; the launch traced here: 104 us
  Pallas kernels  101 us (96%)
  local copies, waits for them, and re-layouts  1.38 us (1%)
  between operations  1.36 us (1%)
    pallas_call x1, Pallas kernels, scatter(): pl.pallas_call(scatter_kernel, out_shape=(jax.ShapeDtypeStruct((FC, ROWS)...  33.2 us
    pallas_call x1, Pallas kernels, gather(): pl.pallas_call(gather_kernel, out_shape=(OUT((NY, NZ, TPN, FC, TILE), BF)...  29.9 us
    pallas_call x1, Pallas kernels, dense(): pl.pallas_call(dense_kernel, out_shape=(jax.ShapeDtypeStruct((FC, ROWS),...  26.5 us
    pallas_call x1, Pallas kernels, backward(): pl.pallas_call(backward_kernel, out_shape=(OUT((NY, NZ, TPN, FC, TILE), B...  6.61 us
    pallas_call x1, Pallas kernels, forward(): pl.pallas_call(forward_kernel, out_shape=OUT((NX, TPN, FC + CNT, TILE), F...  5.05 us

profile of v3, /device:TPU:24, one launch (start us, length us, event | category | flops | bytes accessed | tf_op | source)
XLA Modules:
  0.0 104.0 jit_solution(12726102756207753183)
XLA Ops:
  1.3 29.9 %gather.1 = (bf16[2,8,8,64,128]{4,3,2,1,0:T(8,128)(2,1)S(1)}, bf16[4,64,1024]{2,1,0:T(8,128)(2,1)S(1)}, bf16[4,2,64,256]{3,2,1,0:T(8,128)(2,1)S(1)}, s16[4,256,16,128]{3,2,1,0:T(8,128)(2,1)S(1)}, s32[16,128]{1,0:T(8,128)S(1)}) custom-call(bf16[64,1024]{1,0:T(8,128)(2,1)} %bitcast.8, bf16[64,256]{1,0:T(8,128)(2,1)} %wself.3, bf16[64,256]{1,0:T(8,128)(2,1)} %wneigh.3, ...), custom_call_target="tpu_custom_call" | custom-call | tf_op jit(solution)/shard_map/gather/pallas_call | solution.py:327
  31.1 0.0 copy-start
  31.2 0.0 copy-start.1
  31.2 0.0 copy-start.2
  31.2 5.0 %forward_sums.1.part = f32[4,8,80,128]{3,2,1,0:T(8,128)S(1)} custom-call(s32[16,128]{1,0:T(8,128)S(1)} %get-tuple-element.17.slots, s16[4,256,16,128]{3,2,1,0:T(8,128)(2,1)S(1)} %get-tuple-element.18.edges, bf16[2,8,8,64,128]{4,3,2,1,0:T(8,128)(2,1)S(1)} %get-tuple-element.19.full), custom_call_target="tpu_custom_call" | custom-call | tf_op jit(solution)/shard_map/forward_sums/pallas_call | solution.py:383
  36.2 0.0 copy-done
  36.2 0.0 copy-done.1
  36.3 0.0 copy-done.2
  36.3 26.5 %dense.1 = (f32[64,1024]{1,0:T(8,128)S(1)}, f32[64,1024]{1,0:T(8,128)S(1)}, bf16[4,8,64,128]{3,2,1,0:T(8,128)(2,1)S(1)}, f32[128,256]{1,0:T(8,128)S(1)}) custom-call(f32[4,8,80,128]{3,2,1,0:T(8,128)S(1)} %forward_sums.1.part, bf16[4,64,1024]{2,1,0:T(8,128)(2,1)S(1)} %get-tuple-element.20.xfull, bf16[4,2,64,256]{3,2,1,0:T(8,128)(2,1)S(1)} %get-tuple-element.21.wfull, ...), custom_call_target="tpu_custom_call" | custom-call | tf_op jit(solution)/shard_map/dense/pallas_call | solution.py:525
  62.8 6.6 %backward_sums.1 = (bf16[2,8,8,64,128]{4,3,2,1,0:T(8,128)(2,1)S(1)}, f32[64,1024]{1,0:T(8,128)}) custom-call(s32[16,128]{1,0:T(8,128)S(1)} %get-tuple-element.17.slots, s16[4,256,16,128]{3,2,1,0:T(8,128)(2,1)S(1)} %get-tuple-element.18.edges, bf16[4,8,64,128]{3,2,1,0:T(8,128)(2,1)S(1)} %get-tuple-element.22.source, f32[64,1024]{1,0:T(8,128)S(1)} %get-tuple-element.23.act), custom_call_target="tpu_custom_call" | custom-call | tf_op jit(solution)/shard_map/backward_sums/pallas_call | solution.py:568
  69.4 33.2 %scatter.1 = (f32[64,1024]{1,0:T(8,128)S(1)}, f32[128,256]{1,0:T(8,128)S(1)}) custom-call(bf16[2,8,8,64,128]{4,3,2,1,0:T(8,128)(2,1)S(1)} %get-tuple-element.25.part, f32[128,256]{1,0:T(8,128)S(1)} %get-tuple-element.26.wgrad, f32[64,1024]{1,0:T(8,128)S(1)} %get-tuple-element.27.direct), custom_call_target="tpu_custom_call" | custom-call | tf_op jit(solution)/shard_map/scatter/pallas_call | solution.py:728
  102.6 0.7 fusion
  103.3 0.7 copy.14
Async XLA Ops:
  31.1 5.1 %copy-start = (f32[1024,64]{0,1:T(8,128)S(1)}, f32[1024,64]{0,1:T(8,128)}, u32[]{:S(2)}) copy-start(f32[1024,64]{0,1:T(8,128)} %param.15) | copy-start | bytes 786436
  31.2 5.1 %copy-start.1 = (bf16[64,256]{1,0:T(8,128)(2,1)S(1)}, bf16[64,256]{1,0:T(8,128)(2,1)}, u32[]{:S(2)}) copy-start(bf16[64,256]{1,0:T(8,128)(2,1)} %wself.3) | copy-start | bytes 98308
  31.2 5.1 %copy-start.2 = (bf16[64,256]{1,0:T(8,128)(2,1)S(1)}, bf16[64,256]{1,0:T(8,128)(2,1)}, u32[]{:S(2)}) copy-start(bf16[64,256]{1,0:T(8,128)(2,1)} %wneigh.3) | copy-start | bytes 98308

commit v4 on v3

--- a/solution.py
+++ b/solution.py
@@ -17,6 +17,7 @@
 WORDS = 16
 CNT = 16
 BOTH = (1, -1)
+PARTS = 4
 UNROLL = 8
 HBM = pl.BlockSpec(memory_space=pltpu.HBM)
 VMEM = pl.BlockSpec(memory_space=pltpu.VMEM)
@@ -390,12 +391,18 @@
     )(slots, edges, full)
 
 
+DENSE = (
+    "a0", "a1", "b0", "a2", "b1", "g0", "a3", "b2", "g1", "h0",
+    "b3", "g2", "h1", "s0", "g3", "h2", "s1", "h3", "s2", "s3",
+)
+
+
 def dense_kernel(part, xfull, wfull, wself, wneigh, cot, act, direct, scaled, wgrad,
                  pq, pm, rq, rm, av, gr, send, recv, rs, rr, ss, sr):
     y, z, x, feat = place()
     node = node_of(y, z, x)
-    HALF = TPN // 2
-    SPAN = ROWS // 2
+    CT = TPN // PARTS
+    SPAN = ROWS // PARTS
 
     def xof(k):
         return lax.rem(x + k + 2 * NX, NX)
@@ -410,13 +417,13 @@
 
     def pack(c, k):
         block = xof(k)
-        for q in range(HALF):
-            r = c * HALF + q
+        for q in range(CT):
+            r = c * CT + q
             sums = part[block, r, 0:FC]
             most = jnp.maximum(jnp.max(jnp.abs(sums), axis=0, keepdims=True), 1e-30)
             pq[c, k - 1, q] = jnp.round(sums * (32766.0 / most)).astype(jnp.int32).astype(jnp.int16)
             pm[c, k - 1, q:q + 1] = most * (1.0 / 32766.0)
-            pm[c, k - 1, HALF + q:HALF + q + 1] = part[block, r, FC:FC + 1]
+            pm[c, k - 1, CT + q:CT + q + 1] = part[block, r, FC:FC + 1]
 
     def hop(c, k, what):
         i = (c, k - 1, what)
@@ -427,10 +434,10 @@
     for k in ORDER:
         pack(0, k)
     pl.semaphore_wait(barrier, len(peers))
-    for c in range(2):
+    for c in range(PARTS):
         for k in ORDER:
-            if c == 1:
-                pack(1, k)
+            if c > 0:
+                pack(c, k)
             hop(c, k, 1).start()
             hop(c, k, 0).start()
 
@@ -444,29 +451,29 @@
         pre += dot(cols_of(k, 0), xfull[k])
     neigh = [cols_of(k, 1) for k in range(4)]
 
-    def share(ref, sems, c):
-        return exchange(ref.at[feat, c], lambda k: ref.at[k, c], feat, node, sems, send, recv)
-
-    degrees, first = [], []
-    for c in range(2):
+    def share(ref, stage, c):
+        return exchange(
+            ref.at[feat, c], lambda k: ref.at[k, c], feat, node, 3 * (stage * PARTS + c), send, recv
+        )
+
+    degrees, first, second = {}, {}, {}
+
+    def average(c):
         for k in ORDER:
             for what in (1, 0):
                 hop(c, k, what).wait_recv()
-        for q in range(HALF):
-            r = c * HALF + q
+        for q in range(CT):
+            r = c * CT + q
             total = part[x, r, 0:FC]
             degree = part[x, r, FC:FC + 1]
             for k in range(3):
                 total += rq[c, k, q].astype(jnp.int32).astype(F32) * rm[c, k, q:q + 1]
-                degree += rm[c, k, HALF + q:HALF + q + 1]
-            degree = jnp.maximum(degree, 1.0)
-            degrees.append(degree)
-            av[feat, c, :, q * TILE:(q + 1) * TILE] = (total / degree).astype(BF)
-        first.append(share(av, 3 * c, c))
-    for step, _ in first:
-        step()
-    second = []
-    for c in range(2):
+                degree += rm[c, k, CT + q:CT + q + 1]
+            degrees[r] = jnp.maximum(degree, 1.0)
+            av[feat, c, :, q * TILE:(q + 1) * TILE] = (total / degrees[r]).astype(BF)
+        first[c] = share(av, 0, c)
+
+    def gradient(c):
         first[c][1]()
         span = slice(c * SPAN, (c + 1) * SPAN)
         own = pre[:, span]
@@ -475,47 +482,46 @@
         sig = jax.nn.sigmoid(own)
         grad = cot[:, span] * sig * (1.0 + own * (1.0 - sig))
         gr[feat, c] = grad.astype(BF)
-        second.append(share(gr, 6 + 3 * c, c))
+        second[c] = share(gr, 1, c)
         act[:, span] = own * sig
-    for step, _ in second:
-        step()
-
-    def shop(s, c, d, arriving=False):
-        i = (side(s), c, d - 1)
-        at = scaled.at[xof(-s * d if arriving else -s * (d - 1)), pl.ds(c * HALF, HALF)]
-        return remote(at, at, ss.at[i], sr.at[i], xdev(s))
-
-    for c in range(2):
+
+    def shop(c, k, arriving=False):
+        at = scaled.at[xof(-k) if arriving else x, pl.ds(c * CT, CT)]
+        return remote(at, at, ss.at[c, k - 1], sr.at[c, k - 1], xdev(k))
+
+    def scale(c):
         second[c][1]()
         sums = dot(wneigh[:, 0:FC], gr[0, c])
         for k in range(1, 4):
             sums += dot(wneigh[:, k * FC:(k + 1) * FC], gr[k, c])
-        for q in range(HALF):
-            r = c * HALF + q
+        for q in range(CT):
+            r = c * CT + q
             scaled[x, r] = (sums[:, q * TILE:(q + 1) * TILE] / degrees[r]).astype(BF)
-        for s in BOTH:
-            shop(s, c, 1).start()
-    for c in range(2):
-        straight = dot(wself[:, 0:FC], gr[0, c])
+        for k in ORDER:
+            shop(c, k).start()
+
+    steps = {
+        "a": average, "b": lambda c: first[c][0](), "g": gradient, "h": lambda c: second[c][0](), "s": scale
+    }
+    for step in DENSE:
+        steps[step[0]](int(step[1]))
+    for c in range(PARTS):
+        total = dot(wself[:, 0:FC], gr[0, c])
         for k in range(1, 4):
-            straight += dot(wself[:, k * FC:(k + 1) * FC], gr[k, c])
-        direct[:, c * SPAN:(c + 1) * SPAN] = straight
-    for c in range(2):
-        for s in BOTH:
-            shop(s, c, 1, True).wait_recv()
-            if c == side(s):
-                shop(s, c, 2).start()
+            total += dot(wself[:, k * FC:(k + 1) * FC], gr[k, c])
+        direct[:, c * SPAN:(c + 1) * SPAN] = total
     for k in range(4):
         lanes = slice(k * FC, (k + 1) * FC)
-        wgrad[0:FC, lanes] = nt(xfull[feat, :, 0:SPAN], gr[k, 0]) + nt(xfull[feat, :, SPAN:ROWS], gr[k, 1])
-        wgrad[FC:2 * FC, lanes] = nt(av[feat, 0], gr[k, 0]) + nt(av[feat, 1], gr[k, 1])
-    for s in BOTH:
-        shop(s, side(s), 2, True).wait_recv()
-        shop(s, side(s), 2).wait_send()
-        for c in range(2):
-            shop(s, c, 1).wait_send()
-    for c in range(2):
+        mine, near = jnp.zeros((FC, FC), F32), jnp.zeros((FC, FC), F32)
+        for c in range(PARTS):
+            mine += nt(xfull[feat, :, c * SPAN:(c + 1) * SPAN], gr[k, c])
+            near += nt(av[feat, c], gr[k, c])
+        wgrad[0:FC, lanes] = mine
+        wgrad[FC:2 * FC, lanes] = near
+    for c in range(PARTS):
         for k in ORDER:
+            shop(c, k, True).wait_recv()
+            shop(c, k).wait_send()
             for what in range(2):
                 hop(c, k, what).wait_send()
 
@@ -533,10 +539,11 @@
         in_specs=[VMEM] * 6,
         out_specs=(VMEM,) * 4,
         scratch_shapes=[
-            pltpu.VMEM((2, 3, TPN // 2, FC, TILE), jnp.int16), pltpu.VMEM((2, 3, 8, TILE), F32),
-            pltpu.VMEM((2, 3, TPN // 2, FC, TILE), jnp.int16), pltpu.VMEM((2, 3, 8, TILE), F32),
-            pltpu.VMEM((4, 2, FC, ROWS // 2), BF), pltpu.VMEM((4, 2, FC, ROWS // 2), BF),
-            dma((12,)), dma((12,)), dma((2, 3, 2)), dma((2, 3, 2)), dma((2, 2, 2)), dma((2, 2, 2)),
+            pltpu.VMEM((PARTS, 3, TPN // PARTS, FC, TILE), jnp.int16), pltpu.VMEM((PARTS, 3, 8, TILE), F32),
+            pltpu.VMEM((PARTS, 3, TPN // PARTS, FC, TILE), jnp.int16), pltpu.VMEM((PARTS, 3, 8, TILE), F32),
+            pltpu.VMEM((4, PARTS, FC, ROWS // PARTS), BF), pltpu.VMEM((4, PARTS, FC, ROWS // PARTS), BF),
+            dma((6 * PARTS,)), dma((6 * PARTS,)), dma((PARTS, 3, 2)), dma((PARTS, 3, 2)),
+            dma((PARTS, 3)), dma((PARTS, 3)),
         ],
         compiler_params=pltpu.CompilerParams(
             collective_id=1, has_side_effects=True, vmem_limit_bytes=24 * 2**20
@@ -576,11 +583,14 @@
     )(slots, edges, source, act)
 
 
-def scatter_kernel(part, wgrad, direct, out, wout, rz, ry, rl, w1, w2, zs, zr, ys, yr, ws, wr):
+W_AT = ((4, 0), (3, 0), (2, 0))
+NEAR = 3
+
+
+def scatter_kernel(part, wgrad, direct, out, wout, rz, ry, rl, w1, w2, w3, w4, zs, zr, ys, yr, ws, wr):
     y, z, x, feat = place()
     oy = 1 - y
-    HALF = TPN // 2
-    CUT = HALF // 2
+    FAR = TPN - NEAR
 
     def zof(k):
         return lax.rem(z + k + 2 * NZ, NZ)
@@ -600,45 +610,76 @@
     def term(u, k):
         if u == 2:
             return ry.at[(k + NZ) % NZ]
-        return part.at[oy if u == 1 else y, zof(k), pl.ds(0, HALF)]
+        return part.at[oy if u == 1 else y, zof(k), pl.ds(0, NEAR)]
+
+    def size(u):
+        return FAR if u == 2 else NEAR
+
+    def cut(u, k):
+        return pl.ds(0, 2) if k == 0 else pl.ds(2, size(u) - 2)
+
+    def slot(s, u, d):
+        return rz.at[side(s), u, d - 1, pl.ds(0, size(u))]
 
     def hop(s, u, d):
         i = (side(s), u, d - 1)
+        src, dst = term(u, 4) if d == 4 else slot(s, u, d + 1), slot(s, u, d)
         if d == 4:
-            cut = pl.ds(side(s) * CUT, CUT)
-            return remote(term(u, 4).at[cut], rz.at[i].at[cut], zs.at[i], zr.at[i], zdev(s))
-        return remote(rz.at[side(s), u, d], rz.at[i], zs.at[i], zr.at[i], zdev(s))
+            src, dst = src.at[cut(u, side(s))], dst.at[cut(u, side(s))]
+        return remote(src, dst, zs.at[i], zr.at[i], zdev(s))
 
     def yhop(k):
-        return remote(part.at[oy, zof(k), pl.ds(HALF, HALF)], ry.at[(k + NZ) % NZ],
+        return remote(part.at[oy, zof(k), pl.ds(NEAR, FAR)], ry.at[(k + NZ) % NZ],
                       ys.at[(k + NZ) % NZ], yr.at[(k + NZ) % NZ], ydev)
 
     def join(k):
         yhop(k).wait_recv()
         at = (k + NZ) % NZ
-        ry[at] = (ry[at].astype(F32) + part[y, zof(k), HALF:TPN].astype(F32)).astype(BF)
-
-    last = remote(rz.at[0, 1, 0], rl, ys.at[NZ], yr.at[NZ], ydev)
+        ry[at] = (ry[at].astype(F32) + part[y, zof(k), NEAR:TPN].astype(F32)).astype(BF)
+
+    last = remote(slot(1, 1, 1), rl, ys.at[NZ], yr.at[NZ], ydev)
+
+    def rows(p):
+        return pl.ds(pl.multiple_of(p * 16, 16), 16)
+
+    def pof(k):
+        return lax.rem(plane + k + NY * NX, NY * NX)
 
     def wcopy(phase, k):
         i = phase * 7 + k - 1
-        if phase == 0:
-            return remote(wgrad.at[pl.ds(pl.multiple_of(zof(k) * 16, 16), 16)], w1.at[k - 1], ws.at[i], wr.at[i], zdev(k))
-        if phase == 1:
-            return remote(w2.at[plane], w2.at[plane], ws.at[i], wr.at[i], pdev(k))
-        rows = pl.ds(pl.multiple_of(z * 16, 16), 16)
-        return remote(wout.at[rows], wout.at[rows], ws.at[i], wr.at[i], zdev(k))
+        peer = pdev(k) if phase in (0, 3) else zdev(k)
+        src, dst = (
+            (wgrad.at[rows(pof(k))], w1.at[k - 1]), (w2.at[zof(k)], w3.at[k - 1]), (w4.at[z], w4.at[z]),
+            (wout.at[rows(plane)], wout.at[rows(plane)]),
+        )[phase]
+        return remote(src, dst, ws.at[i], wr.at[i], peer)
 
     def wexpect(phase, k):
         i = phase * 7 + k - 1
+        dst = (w1.at[k - 1], w3.at[k - 1], w4.at[zof(-k)], wout.at[rows(pof(-k))])[phase]
+        return remote(dst, dst, ws.at[i], wr.at[i], zdev(k))
+
+    def wturn(phase):
+        for k in range(1, 8):
+            wexpect(phase, k).wait_recv()
         if phase == 0:
-            dst = w1.at[k - 1]
+            acc = wgrad[rows(plane)]
+            for k in range(1, 8):
+                acc += w1[k - 1]
+            for q in range(NZ):
+                w2[q] = acc[2 * q:2 * q + 2]
         elif phase == 1:
-            dst = w2.at[lax.rem(plane + NY * NX - k, NY * NX)]
+            acc = w2[z]
+            for k in range(1, 8):
+                acc += w3[k - 1]
+            w4[z] = acc
         else:
-            dst = wout.at[pl.ds(pl.multiple_of(zof(-k) * 16, 16), 16)]
-        return remote(dst, dst, ws.at[i], wr.at[i], zdev(k))
-
+            wout[rows(plane)] = jnp.concatenate([w4[q] for q in range(NZ)], axis=0)
+        for k in range(1, 8):
+            wcopy(phase + 1, k).start()
+
+    for k in range(1, 8):
+        wcopy(0, k).start()
     for k in (4, 3, -3):
         yhop(k).start()
     for u in (1, 0):
@@ -646,8 +687,6 @@
             hop(s, u, 4).start()
     for k in (2, -2, 1, -1, 0):
         yhop(k).start()
-    for k in range(1, NZ):
-        wcopy(0, k).start()
     join(4)
     for s in BOTH:
         hop(s, 2, 4).start()
@@ -661,56 +700,41 @@
                 i = (side(s), u, d - 1)
                 more = term(u, s * (d - 1))
                 if d == 4:
-                    a, b = pl.ds(side(s) * CUT, CUT), pl.ds((1 - side(s)) * CUT, CUT)
+                    a, b = cut(u, side(s)), cut(u, 1 - side(s))
                     rz[(*i, a)] = (rz[(*i, a)].astype(F32) + more[a].astype(F32)).astype(BF)
                     rz[(*i, b)] = more[b]
                 else:
+                    i = (*i, slice(0, size(u)))
                     rz[i] = (rz[i].astype(F32) + more[...].astype(F32)).astype(BF)
                 hop(s, u, d - 1).start()
-        if d == 4:
-            for k in range(1, NZ):
-                wexpect(0, k).wait_recv()
-            acc = wgrad[pl.ds(pl.multiple_of(z * 16, 16), 16)]
-            for k in range(1, NZ):
-                acc += w1[k - 1]
-            w2[plane] = acc
-            for k in range(1, NY * NX):
-                wcopy(1, k).start()
-        if d == 3:
-            for k in range(1, NY * NX):
-                wexpect(1, k).wait_recv()
-            acc = w2[0]
-            for k in range(1, NY * NX):
-                acc += w2[k]
-            wout[pl.ds(pl.multiple_of(z * 16, 16), 16)] = acc
-            for k in range(1, NZ):
-                wcopy(2, k).start()
+            if (d, u) in W_AT:
+                wturn(W_AT.index((d, u)))
 
     def total(u):
         for s in BOTH:
             hop(s, u, 1).wait_recv()
-        return term(u, 0)[...].astype(F32) + rz[0, u, 0].astype(F32) + rz[1, u, 0].astype(F32)
-
-    perm = order().astype(F32)
-
-    def finish(t, sums):
-        back = jnp.dot(sums, perm, preferred_element_type=F32, precision=lax.Precision.HIGHEST)
-        lanes = slice(t * TILE, (t + 1) * TILE)
-        out[:, lanes] = direct[:, lanes] + back
-
-    rz[0, 1, 0] = total(1).astype(BF)
+        one, two = rz[0, u, 0, 0:size(u)].astype(F32), rz[1, u, 0, 0:size(u)].astype(F32)
+        return term(u, 0)[...].astype(F32) + one + two
+
+    perm = order()
+
+    def finish(base, sums):
+        flat = sums.reshape(-1, TILE)
+        high = flat.astype(BF)
+        back = dot(high, perm) + dot((flat - high.astype(F32)).astype(BF), perm)
+        for t in range(sums.shape[0]):
+            lanes = slice((base + t) * TILE, (base + t + 1) * TILE)
+            out[:, lanes] = direct[:, lanes] + back[t * FC:(t + 1) * FC]
+
+    rz[0, 1, 0, 0:NEAR] = total(1).astype(BF)
     last.start()
     join(0)
-    sums = total(2)
-    for t in range(HALF):
-        finish(HALF + t, sums[t])
+    finish(NEAR, total(2))
     sums = total(0)
     last.wait_recv()
-    sums += rl[...].astype(F32)
-    for t in range(HALF):
-        finish(t, sums[t])
+    finish(0, sums + rl[...].astype(F32))
     for k in range(1, NZ):
-        wexpect(2, k).wait_recv()
+        wexpect(3, k).wait_recv()
     for s in BOTH:
         for u in range(3):
             for d in range(1, 5):
@@ -718,7 +742,7 @@
     for k in range(NZ):
         yhop(k).wait_send()
     last.wait_send()
-    for phase in range(3):
+    for phase in range(4):
         for k in range(1, 8):
             wcopy(phase, k).wait_send()
 
@@ -734,12 +758,12 @@
         in_specs=[VMEM, VMEM, VMEM],
         out_specs=(VMEM, VMEM),
         scratch_shapes=[
-            pltpu.VMEM((2, 3, 4, TPN // 2, FC, TILE), BF),
-            pltpu.VMEM((NZ, TPN // 2, FC, TILE), BF),
-            pltpu.VMEM((TPN // 2, FC, TILE), BF),
+            pltpu.VMEM((2, 3, 4, TPN - NEAR, FC, TILE), BF),
+            pltpu.VMEM((NZ, TPN - NEAR, FC, TILE), BF),
+            pltpu.VMEM((NEAR, FC, TILE), BF),
             pltpu.VMEM((NZ - 1, 16, 256), F32),
-            pltpu.VMEM((NY * NX, 16, 256), F32),
-            dma((2, 3, 4)), dma((2, 3, 4)), dma((NZ + 1,)), dma((NZ + 1,)), dma((21,)), dma((21,)),
+            pltpu.VMEM((NZ, 2, 256), F32), pltpu.VMEM((NZ - 1, 2, 256), F32), pltpu.VMEM((NZ, 2, 256), F32),
+            dma((2, 3, 4)), dma((2, 3, 4)), dma((NZ + 1,)), dma((NZ + 1,)), dma((28,)), dma((28,)),
         ],
         compiler_params=pltpu.CompilerParams(
             collective_id=2, has_side_effects=True, vmem_limit_bytes=24 * 2**20

time: 105 us -> 104 us (level)
  Pallas kernels: 101 us -> 99.8 us
where the time goes in v4:
time: 104 us; the launch traced here: 102 us
  Pallas kernels  99.8 us (96%)
  local copies, waits for them, and re-layouts  1.38 us (1%)
  between operations  1.36 us (1%)
    pallas_call x1, Pallas kernels, scatter(): pl.pallas_call(scatter_kernel, out_shape=(jax.ShapeDtypeStruct((FC, ROWS)...  33 us
    pallas_call x1, Pallas kernels, gather(): pl.pallas_call(gather_kernel, out_shape=(OUT((NY, NZ, TPN, FC, TILE), BF)...  29.9 us
    pallas_call x1, Pallas kernels, dense(): pl.pallas_call(dense_kernel, out_shape=(jax.ShapeDtypeStruct((FC, ROWS),...  25.8 us
    pallas_call x1, Pallas kernels, backward(): pl.pallas_call(backward_kernel, out_shape=(OUT((NY, NZ, TPN, FC, TILE), B...  6.32 us
    pallas_call x1, Pallas kernels, forward(): pl.pallas_call(forward_kernel, out_shape=OUT((NX, TPN, FC + CNT, TILE), F...  4.8 us

profile of v4, /device:TPU:24, one launch (start us, length us, event | category | flops | bytes accessed | tf_op | source)
XLA Modules:
  0.0 102.5 jit_solution(6260865349176735273)
XLA Ops:
  1.3 29.9 %gather.1 = (bf16[2,8,8,64,128]{4,3,2,1,0:T(8,128)(2,1)S(1)}, bf16[4,64,1024]{2,1,0:T(8,128)(2,1)S(1)}, bf16[4,2,64,256]{3,2,1,0:T(8,128)(2,1)S(1)}, s16[4,256,16,128]{3,2,1,0:T(8,128)(2,1)S(1)}, s32[16,128]{1,0:T(8,128)S(1)}) custom-call(bf16[64,1024]{1,0:T(8,128)(2,1)} %bitcast.8, bf16[64,256]{1,0:T(8,128)(2,1)} %wself.3, bf16[64,256]{1,0:T(8,128)(2,1)} %wneigh.3, ...), custom_call_target="tpu_custom_call" | custom-call | tf_op jit(solution)/shard_map/gather/pallas_call | solution.py:328
  31.1 0.0 copy-start
  31.2 0.0 copy-start.1
  31.2 0.0 copy-start.2
  31.2 4.8 %forward_sums.1.part = f32[4,8,80,128]{3,2,1,0:T(8,128)S(1)} custom-call(s32[16,128]{1,0:T(8,128)S(1)} %get-tuple-element.17.slots, s16[4,256,16,128]{3,2,1,0:T(8,128)(2,1)S(1)} %get-tuple-element.18.edges, bf16[2,8,8,64,128]{4,3,2,1,0:T(8,128)(2,1)S(1)} %get-tuple-element.19.full), custom_call_target="tpu_custom_call" | custom-call | tf_op jit(solution)/shard_map/forward_sums/pallas_call | solution.py:384
  36.0 0.0 copy-done
  36.0 0.0 copy-done.1
  36.0 0.0 copy-done.2
  36.0 25.8 %dense.1 = (f32[64,1024]{1,0:T(8,128)S(1)}, f32[64,1024]{1,0:T(8,128)S(1)}, bf16[4,8,64,128]{3,2,1,0:T(8,128)(2,1)S(1)}, f32[128,256]{1,0:T(8,128)S(1)}) custom-call(f32[4,8,80,128]{3,2,1,0:T(8,128)S(1)} %forward_sums.1.part, bf16[4,64,1024]{2,1,0:T(8,128)(2,1)S(1)} %get-tuple-element.20.xfull, bf16[4,2,64,256]{3,2,1,0:T(8,128)(2,1)S(1)} %get-tuple-element.21.wfull, ...), custom_call_target="tpu_custom_call" | custom-call | tf_op jit(solution)/shard_map/dense/pallas_call | solution.py:531
  61.8 6.3 %backward_sums.1 = (bf16[2,8,8,64,128]{4,3,2,1,0:T(8,128)(2,1)S(1)}, f32[64,1024]{1,0:T(8,128)}) custom-call(s32[16,128]{1,0:T(8,128)S(1)} %get-tuple-element.17.slots, s16[4,256,16,128]{3,2,1,0:T(8,128)(2,1)S(1)} %get-tuple-element.18.edges, bf16[4,8,64,128]{3,2,1,0:T(8,128)(2,1)S(1)} %get-tuple-element.22.source, f32[64,1024]{1,0:T(8,128)S(1)} %get-tuple-element.23.act), custom_call_target="tpu_custom_call" | custom-call | tf_op jit(solution)/shard_map/backward_sums/pallas_call | solution.py:575
  68.1 33.0 %scatter.1 = (f32[64,1024]{1,0:T(8,128)S(1)}, f32[128,256]{1,0:T(8,128)S(1)}) custom-call(bf16[2,8,8,64,128]{4,3,2,1,0:T(8,128)(2,1)S(1)} %get-tuple-element.25.part, f32[128,256]{1,0:T(8,128)S(1)} %get-tuple-element.26.wgrad, f32[64,1024]{1,0:T(8,128)S(1)} %get-tuple-element.27.direct), custom_call_target="tpu_custom_call" | custom-call | tf_op jit(solution)/shard_map/scatter/pallas_call | solution.py:752
  101.1 0.7 fusion
  101.8 0.7 copy.14
Async XLA Ops:
  31.1 4.8 %copy-start = (f32[1024,64]{0,1:T(8,128)S(1)}, f32[1024,64]{0,1:T(8,128)}, u32[]{:S(2)}) copy-start(f32[1024,64]{0,1:T(8,128)} %param.15) | copy-start | bytes 786436
  31.2 4.8 %copy-start.1 = (bf16[64,256]{1,0:T(8,128)(2,1)S(1)}, bf16[64,256]{1,0:T(8,128)(2,1)}, u32[]{:S(2)}) copy-start(bf16[64,256]{1,0:T(8,128)(2,1)} %wself.3) | copy-start | bytes 98308
  31.2 4.8 %copy-start.2 = (bf16[64,256]{1,0:T(8,128)(2,1)S(1)}, bf16[64,256]{1,0:T(8,128)(2,1)}, u32[]{:S(2)}) copy-start(bf16[64,256]{1,0:T(8,128)(2,1)} %wneigh.3) | copy-start | bytes 98308

commit v5 on v4

--- a/solution.py
+++ b/solution.py
@@ -15,6 +15,7 @@
 ROWS = TPN * TILE
 SLOTS = 256
 WORDS = 16
+LISTED = 9
 CNT = 16
 BOTH = (1, -1)
 PARTS = 4
@@ -272,17 +273,30 @@
         row = lax.shift_right_logical(slot, 8) * TPN + jnp.bitwise_and(lax.shift_right_arithmetic(code, 16), 7)
         near = lax.shift_left(lax.shift_right_logical(col, 5), 3) + jnp.bitwise_and(col, 7)
         upto = jnp.where(iota((TILE, TILE), 0) <= iota((TILE, TILE), 1), 1.0, 0.0).astype(BF)
-        prefix = dot(mine.astype(BF), upto)
-        pos = jnp.where(mine > 0.0, prefix - 1.0, -1.0e6)
-        base = jnp.zeros((1, 1), F32)
-        shifted = []
-        for r in range(8):
-            shifted.append(pos[r:r + 1] + base)
-            base = base + prefix[r:r + 1, TILE - 1:TILE]
-        pos = jnp.concatenate(shifted + [jnp.zeros((TILE - 8, TILE), F32)], axis=0).T
-        wide = iota((TILE, 8 * TILE), 1).astype(F32)
-        picked = jnp.zeros((8, 8 * TILE), F32)
-        fields = (jnp.bitwise_and(slot, 255), lax.shift_right_logical(slot, 8), row, near)
+        tile = jnp.bitwise_and(row, 7)
+        runs, begin, places = [], jnp.zeros((1, TILE), F32), []
+        for b in range(NX):
+            seen = jnp.zeros((TPN, 1), F32)
+            for r in (2 * b, 2 * b + 1):
+                hot = jnp.where(iota((TPN, TILE), 0) == tile[r:r + 1], mine[r:r + 1], 0.0)
+                rank = dot(hot.astype(BF), upto) + seen
+                runs.append((hot, rank))
+                seen = rank[:, TILE - 1:TILE]
+            even = jnp.broadcast_to(2.0 * jnp.floor((seen + 1.0) * 0.5), (TPN, TILE))
+            starts = []
+            for j in range(TPN):
+                starts.append(begin)
+                begin = begin + even[j:j + 1]
+            start = jnp.concatenate(starts, axis=0) - 1.0
+            for r in (2 * b, 2 * b + 1):
+                hot, rank = runs[r]
+                place = jnp.sum(hot * (start + rank), axis=0, keepdims=True)
+                places.append(jnp.where(mine[r:r + 1] > 0.0, place, -1.0e6))
+        base = begin
+        pos = jnp.concatenate(places + [jnp.zeros((TILE - 8, TILE), F32)], axis=0).T
+        wide = iota((TILE, LISTED * TILE), 1).astype(F32)
+        picked = jnp.zeros((8, LISTED * TILE), F32)
+        fields = (jnp.bitwise_and(slot, 255), lax.shift_right_logical(slot, 8), row, near + 128)
         state.update(pos=pos, base=base, wide=wide, picked=picked, fields=fields)
 
     def pick(r):
@@ -294,9 +308,9 @@
     def enlist():
         picked, base = state["picked"], state["base"]
         items = (picked[0:1] + 256.0 * picked[1:2] + 1024.0 * picked[2:3] + 32768.0 * picked[3:4]).astype(jnp.int32)
-        for r in range(8):
+        for r in range(LISTED):
             listed[r:r + 1] = items[:, r * TILE:(r + 1) * TILE]
-        listed[8:16] = jnp.broadcast_to(base, (8, TILE)).astype(jnp.int32)
+        listed[LISTED:16] = jnp.broadcast_to(base, (16 - LISTED, TILE)).astype(jnp.int32)
 
     steps = {"z": zpass, "e": eround, "h": efar, "s": efirst, "y": ycross, "x": passon, "c": prepare, "l": pick, "i": enlist}
     for step in ORDER:
@@ -356,25 +370,30 @@
     )
 
 
-def entry(slots, group, u, count, edges):
+def entry(slots, group, u, edges):
     item = slots[lax.shift_right_logical(group, 4), jnp.bitwise_and(group, 15) * UNROLL + u]
     words = edges[jnp.bitwise_and(lax.shift_right_logical(item, 8), 3), jnp.bitwise_and(item, 255)]
-    planes = planes_of(jnp.where(group * UNROLL + u < count, words, jnp.zeros_like(words)))
-    return jnp.bitwise_and(lax.shift_right_logical(item, 10), 31), lax.shift_right_logical(item, 15), planes
+    planes = planes_of(jnp.where(item > 0, words, jnp.zeros_like(words)))
+    row, col = lax.shift_right_logical(item, 10), lax.shift_right_logical(item, 15)
+    return jnp.bitwise_and(row, 31), jnp.bitwise_and(col, 127), planes
 
 
 def forward_kernel(slots, edges, full, acc):
     acc[...] = jnp.zeros_like(acc)
-    count = slots[8, 0]
+    count = slots[LISTED, 0]
     ones = jnp.ones((CNT, TILE), BF)
 
+    def source(col):
+        near, t = lax.shift_right_logical(col, 3), jnp.bitwise_and(col, 7)
+        return jnp.concatenate([full[lax.shift_right_logical(near, 3), jnp.bitwise_and(near, 7), t], ones], axis=0)
+
     def group(g, _):
-        for u in range(UNROLL):
-            row, col, planes = entry(slots, g, u, count, edges)
-            near, t = lax.shift_right_logical(col, 3), jnp.bitwise_and(col, 7)
-            block, tile = lax.shift_right_logical(row, 3), jnp.bitwise_and(row, 7)
-            source = full[lax.shift_right_logical(near, 3), jnp.bitwise_and(near, 7), t]
-            acc[block, tile] += dot(jnp.concatenate([source, ones], axis=0), planes)
+        for u in range(0, UNROLL, 2):
+            row, one, first = entry(slots, g, u, edges)
+            _, two, second = entry(slots, g, u + 1, edges)
+            acc[lax.shift_right_logical(row, 3), jnp.bitwise_and(row, 7)] += dot(
+                jnp.concatenate([source(one), source(two)], axis=1), jnp.concatenate([first, second], axis=0)
+            )
         return 0
 
     lax.fori_loop(0, (count + UNROLL - 1) // UNROLL, group, 0)
@@ -555,13 +574,18 @@
 def backward_kernel(slots, edges, source, act, out, acted, acc):
     acted[...] = act[...]
     acc[...] = jnp.zeros_like(acc)
-    count = slots[8, 0]
+    count = slots[LISTED, 0]
 
     def group(g, _):
-        for u in range(UNROLL):
-            row, col, planes = entry(slots, g, u, count, edges)
-            block, tile = lax.shift_right_logical(row, 3), jnp.bitwise_and(row, 7)
-            acc[col] += nt(source[block, tile], planes)
+        for u in range(0, UNROLL, 2):
+            row, one, first = entry(slots, g, u, edges)
+            _, two, second = entry(slots, g, u + 1, edges)
+            sums = nt(
+                source[lax.shift_right_logical(row, 3), jnp.bitwise_and(row, 7)],
+                jnp.concatenate([first, second], axis=0),
+            )
+            acc[one] += sums[:, 0:TILE]
+            acc[two] += sums[:, TILE:2 * TILE]
         return 0
 
     lax.fori_loop(0, (count + UNROLL - 1) // UNROLL, group, 0)

time: 104 us -> 104 us (level)
  no operation moved by 1% of the time
where the time goes in v5:
time: 104 us; the launch traced here: 102 us
  Pallas kernels  99.7 us (96%)
  local copies, waits for them, and re-layouts  1.38 us (1%)
  between operations  1.35 us (1%)
    pallas_call x1, Pallas kernels, scatter(): pl.pallas_call(scatter_kernel, out_shape=(jax.ShapeDtypeStruct((FC, ROWS)...  32.9 us
    pallas_call x1, Pallas kernels, gather(): pl.pallas_call(gather_kernel, out_shape=(OUT((NY, NZ, TPN, FC, TILE), BF)...  29.9 us
    pallas_call x1, Pallas kernels, dense(): pl.pallas_call(dense_kernel, out_shape=(jax.ShapeDtypeStruct((FC, ROWS),...  25.5 us
    pallas_call x1, Pallas kernels, backward(): pl.pallas_call(backward_kernel, out_shape=(OUT((NY, NZ, TPN, FC, TILE), B...  6.12 us
    pallas_call x1, Pallas kernels, forward(): pl.pallas_call(forward_kernel, out_shape=OUT((NX, TPN, FC + CNT, TILE), F...  5.15 us

profile of v5, /device:TPU:24, one launch (start us, length us, event | category | flops | bytes accessed | tf_op | source)
XLA Modules:
  0.0 102.4 jit_solution(6307418146834280350)
XLA Ops:
  1.3 29.9 %gather.1 = (bf16[2,8,8,64,128]{4,3,2,1,0:T(8,128)(2,1)S(1)}, bf16[4,64,1024]{2,1,0:T(8,128)(2,1)S(1)}, bf16[4,2,64,256]{3,2,1,0:T(8,128)(2,1)S(1)}, s16[4,256,16,128]{3,2,1,0:T(8,128)(2,1)S(1)}, s32[16,128]{1,0:T(8,128)S(1)}) custom-call(bf16[64,1024]{1,0:T(8,128)(2,1)} %bitcast.8, bf16[64,256]{1,0:T(8,128)(2,1)} %wself.3, bf16[64,256]{1,0:T(8,128)(2,1)} %wneigh.3, ...), custom_call_target="tpu_custom_call" | custom-call | tf_op jit(solution)/shard_map/gather/pallas_call | solution.py:342
  31.2 0.0 copy-start
  31.2 0.0 copy-start.1
  31.2 0.0 copy-start.2
  31.2 5.2 %forward_sums.1.part = f32[4,8,80,128]{3,2,1,0:T(8,128)S(1)} custom-call(s32[16,128]{1,0:T(8,128)S(1)} %get-tuple-element.17.slots, s16[4,256,16,128]{3,2,1,0:T(8,128)(2,1)S(1)} %get-tuple-element.18.edges, bf16[2,8,8,64,128]{4,3,2,1,0:T(8,128)(2,1)S(1)} %get-tuple-element.19.full), custom_call_target="tpu_custom_call" | custom-call | tf_op jit(solution)/shard_map/forward_sums/pallas_call | solution.py:403
  36.4 0.0 copy-done
  36.4 0.0 copy-done.1
  36.4 0.0 copy-done.2
  36.4 25.5 %dense.1 = (f32[64,1024]{1,0:T(8,128)S(1)}, f32[64,1024]{1,0:T(8,128)S(1)}, bf16[4,8,64,128]{3,2,1,0:T(8,128)(2,1)S(1)}, f32[128,256]{1,0:T(8,128)S(1)}) custom-call(f32[4,8,80,128]{3,2,1,0:T(8,128)S(1)} %forward_sums.1.part, bf16[4,64,1024]{2,1,0:T(8,128)(2,1)S(1)} %get-tuple-element.20.xfull, bf16[4,2,64,256]{3,2,1,0:T(8,128)(2,1)S(1)} %get-tuple-element.21.wfull, ...), custom_call_target="tpu_custom_call" | custom-call | tf_op jit(solution)/shard_map/dense/pallas_call | solution.py:550
  61.9 6.1 %backward_sums.1 = (bf16[2,8,8,64,128]{4,3,2,1,0:T(8,128)(2,1)S(1)}, f32[64,1024]{1,0:T(8,128)}) custom-call(s32[16,128]{1,0:T(8,128)S(1)} %get-tuple-element.17.slots, s16[4,256,16,128]{3,2,1,0:T(8,128)(2,1)S(1)} %get-tuple-element.18.edges, bf16[4,8,64,128]{3,2,1,0:T(8,128)(2,1)S(1)} %get-tuple-element.22.source, f32[64,1024]{1,0:T(8,128)S(1)} %get-tuple-element.23.act), custom_call_target="tpu_custom_call" | custom-call | tf_op jit(solution)/shard_map/backward_sums/pallas_call | solution.py:599
  68.1 32.9 %scatter.1 = (f32[64,1024]{1,0:T(8,128)S(1)}, f32[128,256]{1,0:T(8,128)S(1)}) custom-call(bf16[2,8,8,64,128]{4,3,2,1,0:T(8,128)(2,1)S(1)} %get-tuple-element.25.part, f32[128,256]{1,0:T(8,128)S(1)} %get-tuple-element.26.wgrad, f32[64,1024]{1,0:T(8,128)S(1)} %get-tuple-element.27.direct), custom_call_target="tpu_custom_call" | custom-call | tf_op jit(solution)/shard_map/scatter/pallas_call | solution.py:776
  101.0 0.7 fusion
  101.7 0.7 copy.14
Async XLA Ops:
  31.2 5.2 %copy-start = (f32[1024,64]{0,1:T(8,128)S(1)}, f32[1024,64]{0,1:T(8,128)}, u32[]{:S(2)}) copy-start(f32[1024,64]{0,1:T(8,128)} %param.15) | copy-start | bytes 786436
  31.2 5.2 %copy-start.1 = (bf16[64,256]{1,0:T(8,128)(2,1)S(1)}, bf16[64,256]{1,0:T(8,128)(2,1)}, u32[]{:S(2)}) copy-start(bf16[64,256]{1,0:T(8,128)(2,1)} %wself.3) | copy-start | bytes 98308
  31.2 5.2 %copy-start.2 = (bf16[64,256]{1,0:T(8,128)(2,1)S(1)}, bf16[64,256]{1,0:T(8,128)(2,1)}, u32[]{:S(2)}) copy-start(bf16[64,256]{1,0:T(8,128)(2,1)} %wneigh.3) | copy-start | bytes 98308

commit v6 on v5

--- a/solution.py
+++ b/solution.py
@@ -19,7 +19,8 @@
 CNT = 16
 BOTH = (1, -1)
 PARTS = 4
-UNROLL = 8
+UNROLL = 32
+TURNS = TILE // UNROLL
 HBM = pl.BlockSpec(memory_space=pltpu.HBM)
 VMEM = pl.BlockSpec(memory_space=pltpu.VMEM)
 SMEM = pl.BlockSpec(memory_space=pltpu.SMEM)
@@ -371,7 +372,7 @@
 
 
 def entry(slots, group, u, edges):
-    item = slots[lax.shift_right_logical(group, 4), jnp.bitwise_and(group, 15) * UNROLL + u]
+    item = slots[group // TURNS, lax.rem(group, TURNS) * UNROLL + u]
     words = edges[jnp.bitwise_and(lax.shift_right_logical(item, 8), 3), jnp.bitwise_and(item, 255)]
     planes = planes_of(jnp.where(item > 0, words, jnp.zeros_like(words)))
     row, col = lax.shift_right_logical(item, 10), lax.shift_right_logical(item, 15)

time: 104 us -> 97.2 us (0.935)
  Pallas kernels: 99.7 us -> 92.8 us
    pallas_call x1, Pallas kernels: 32.9 us -> 29.9 us  [scatter(): pl.pallas_call(scatter_kernel, out_shape=(jax.ShapeDtypeStruct((FC, ROWS)...]
    pallas_call x1, Pallas kernels: 6.12 us -> 4.11 us  [backward(): pl.pallas_call(backward_kernel, out_shape=(OUT((NY, NZ, TPN, FC, TILE), B...]
    pallas_call x1, Pallas kernels: 5.15 us -> 3.31 us  [forward(): pl.pallas_call(forward_kernel, out_shape=OUT((NX, TPN, FC + CNT, TILE), F...]
where the time goes in v6:
time: 97.2 us; the launch traced here: 95.5 us
  Pallas kernels  92.8 us (95%)
  local copies, waits for them, and re-layouts  1.38 us (1%)
  between operations  1.35 us (1%)
    pallas_call x1, Pallas kernels, scatter(): pl.pallas_call(scatter_kernel, out_shape=(jax.ShapeDtypeStruct((FC, ROWS)...  29.9 us
    pallas_call x1, Pallas kernels, gather(): pl.pallas_call(gather_kernel, out_shape=(OUT((NY, NZ, TPN, FC, TILE), BF)...  29.9 us
    pallas_call x1, Pallas kernels, dense(): pl.pallas_call(dense_kernel, out_shape=(jax.ShapeDtypeStruct((FC, ROWS),...  25.5 us
    pallas_call x1, Pallas kernels, backward(): pl.pallas_call(backward_kernel, out_shape=(OUT((NY, NZ, TPN, FC, TILE), B...  4.11 us
    pallas_call x1, Pallas kernels, forward(): pl.pallas_call(forward_kernel, out_shape=OUT((NX, TPN, FC + CNT, TILE), F...  3.31 us

profile of v6, /device:TPU:24, one launch (start us, length us, event | category | flops | bytes accessed | tf_op | source)
XLA Modules:
  0.0 95.5 jit_solution(17721144730571428911)
XLA Ops:
  1.3 29.9 %gather.1 = (bf16[2,8,8,64,128]{4,3,2,1,0:T(8,128)(2,1)S(1)}, bf16[4,64,1024]{2,1,0:T(8,128)(2,1)S(1)}, bf16[4,2,64,256]{3,2,1,0:T(8,128)(2,1)S(1)}, s16[4,256,16,128]{3,2,1,0:T(8,128)(2,1)S(1)}, s32[16,128]{1,0:T(8,128)S(1)}) custom-call(bf16[64,1024]{1,0:T(8,128)(2,1)} %bitcast.8, bf16[64,256]{1,0:T(8,128)(2,1)} %wself.3, bf16[64,256]{1,0:T(8,128)(2,1)} %wneigh.3, ...), custom_call_target="tpu_custom_call" | custom-call | tf_op jit(solution)/shard_map/gather/pallas_call | solution.py:343
  31.2 0.0 copy-start
  31.2 0.0 copy-start.1
  31.2 0.0 copy-start.2
  31.2 3.3 %forward_sums.1.part = f32[4,8,80,128]{3,2,1,0:T(8,128)S(1)} custom-call(s32[16,128]{1,0:T(8,128)S(1)} %get-tuple-element.17.slots, s16[4,256,16,128]{3,2,1,0:T(8,128)(2,1)S(1)} %get-tuple-element.18.edges, bf16[2,8,8,64,128]{4,3,2,1,0:T(8,128)(2,1)S(1)} %get-tuple-element.19.full), custom_call_target="tpu_custom_call" | custom-call | tf_op jit(solution)/shard_map/forward_sums/pallas_call | solution.py:404
  34.5 0.0 copy-done
  34.5 0.0 copy-done.1
  34.5 0.0 copy-done.2
  34.6 25.5 %dense.1 = (f32[64,1024]{1,0:T(8,128)S(1)}, f32[64,1024]{1,0:T(8,128)S(1)}, bf16[4,8,64,128]{3,2,1,0:T(8,128)(2,1)S(1)}, f32[128,256]{1,0:T(8,128)S(1)}) custom-call(f32[4,8,80,128]{3,2,1,0:T(8,128)S(1)} %forward_sums.1.part, bf16[4,64,1024]{2,1,0:T(8,128)(2,1)S(1)} %get-tuple-element.20.xfull, bf16[4,2,64,256]{3,2,1,0:T(8,128)(2,1)S(1)} %get-tuple-element.21.wfull, ...), custom_call_target="tpu_custom_call" | custom-call | tf_op jit(solution)/shard_map/dense/pallas_call | solution.py:551
  60.1 4.1 %backward_sums.1 = (bf16[2,8,8,64,128]{4,3,2,1,0:T(8,128)(2,1)S(1)}, f32[64,1024]{1,0:T(8,128)}) custom-call(s32[16,128]{1,0:T(8,128)S(1)} %get-tuple-element.17.slots, s16[4,256,16,128]{3,2,1,0:T(8,128)(2,1)S(1)} %get-tuple-element.18.edges, bf16[4,8,64,128]{3,2,1,0:T(8,128)(2,1)S(1)} %get-tuple-element.22.source, f32[64,1024]{1,0:T(8,128)S(1)} %get-tuple-element.23.act), custom_call_target="tpu_custom_call" | custom-call | tf_op jit(solution)/shard_map/backward_sums/pallas_call | solution.py:600
  64.2 29.9 %scatter.1 = (f32[64,1024]{1,0:T(8,128)S(1)}, f32[128,256]{1,0:T(8,128)S(1)}) custom-call(bf16[2,8,8,64,128]{4,3,2,1,0:T(8,128)(2,1)S(1)} %get-tuple-element.25.part, f32[128,256]{1,0:T(8,128)S(1)} %get-tuple-element.26.wgrad, f32[64,1024]{1,0:T(8,128)S(1)} %get-tuple-element.27.direct), custom_call_target="tpu_custom_call" | custom-call | tf_op jit(solution)/shard_map/scatter/pallas_call | solution.py:777
  94.1 0.7 fusion
  94.8 0.7 copy.14
Async XLA Ops:
  31.2 3.4 %copy-start = (f32[1024,64]{0,1:T(8,128)S(1)}, f32[1024,64]{0,1:T(8,128)}, u32[]{:S(2)}) copy-start(f32[1024,64]{0,1:T(8,128)} %param.15) | copy-start | bytes 786436
  31.2 3.3 %copy-start.1 = (bf16[64,256]{1,0:T(8,128)(2,1)S(1)}, bf16[64,256]{1,0:T(8,128)(2,1)}, u32[]{:S(2)}) copy-start(bf16[64,256]{1,0:T(8,128)(2,1)} %wself.3) | copy-start | bytes 98308
  31.2 3.3 %copy-start.2 = (bf16[64,256]{1,0:T(8,128)(2,1)S(1)}, bf16[64,256]{1,0:T(8,128)(2,1)}, u32[]{:S(2)}) copy-start(bf16[64,256]{1,0:T(8,128)(2,1)} %wneigh.3) | copy-start | bytes 98308

commit v7 on v6

--- a/solution.py
+++ b/solution.py
@@ -19,7 +19,7 @@
 CNT = 16
 BOTH = (1, -1)
 PARTS = 4
-UNROLL = 32
+UNROLL = 64
 TURNS = TILE // UNROLL
 HBM = pl.BlockSpec(memory_space=pltpu.HBM)
 VMEM = pl.BlockSpec(memory_space=pltpu.VMEM)
@@ -466,14 +466,13 @@
     def cols_of(k, which):
         return nt(choose, wfull[k, which]).astype(BF)
 
-    pre = dot(cols_of(0, 0), xfull[0])
-    for k in range(1, 4):
-        pre += dot(cols_of(k, 0), xfull[k])
-    neigh = [cols_of(k, 1) for k in range(4)]
+    itself = jnp.concatenate([cols_of(k, 0) for k in range(4)], axis=1)
+    neigh = jnp.concatenate([cols_of(k, 1) for k in range(4)], axis=1)
+    pre = dot(itself, xfull[...].reshape(4 * FC, ROWS))
 
     def share(ref, stage, c):
         return exchange(
-            ref.at[feat, c], lambda k: ref.at[k, c], feat, node, 3 * (stage * PARTS + c), send, recv
+            ref.at[c, feat], lambda k: ref.at[c, k], feat, node, 3 * (stage * PARTS + c), send, recv
         )
 
     degrees, first, second = {}, {}, {}
@@ -490,18 +489,16 @@
                 total += rq[c, k, q].astype(jnp.int32).astype(F32) * rm[c, k, q:q + 1]
                 degree += rm[c, k, CT + q:CT + q + 1]
             degrees[r] = jnp.maximum(degree, 1.0)
-            av[feat, c, :, q * TILE:(q + 1) * TILE] = (total / degrees[r]).astype(BF)
+            av[c, feat, :, q * TILE:(q + 1) * TILE] = (total / degrees[r]).astype(BF)
         first[c] = share(av, 0, c)
 
     def gradient(c):
         first[c][1]()
         span = slice(c * SPAN, (c + 1) * SPAN)
-        own = pre[:, span]
-        for k in range(4):
-            own += dot(neigh[k], av[k, c])
+        own = pre[:, span] + dot(neigh, av[c].reshape(4 * FC, SPAN))
         sig = jax.nn.sigmoid(own)
         grad = cot[:, span] * sig * (1.0 + own * (1.0 - sig))
-        gr[feat, c] = grad.astype(BF)
+        gr[c, feat] = grad.astype(BF)
         second[c] = share(gr, 1, c)
         act[:, span] = own * sig
 
@@ -511,9 +508,7 @@
 
     def scale(c):
         second[c][1]()
-        sums = dot(wneigh[:, 0:FC], gr[0, c])
-        for k in range(1, 4):
-            sums += dot(wneigh[:, k * FC:(k + 1) * FC], gr[k, c])
+        sums = dot(wneigh[...], gr[c].reshape(4 * FC, SPAN))
         for q in range(CT):
             r = c * CT + q
             scaled[x, r] = (sums[:, q * TILE:(q + 1) * TILE] / degrees[r]).astype(BF)
@@ -526,18 +521,14 @@
     for step in DENSE:
         steps[step[0]](int(step[1]))
     for c in range(PARTS):
-        total = dot(wself[:, 0:FC], gr[0, c])
-        for k in range(1, 4):
-            total += dot(wself[:, k * FC:(k + 1) * FC], gr[k, c])
-        direct[:, c * SPAN:(c + 1) * SPAN] = total
-    for k in range(4):
-        lanes = slice(k * FC, (k + 1) * FC)
-        mine, near = jnp.zeros((FC, FC), F32), jnp.zeros((FC, FC), F32)
-        for c in range(PARTS):
-            mine += nt(xfull[feat, :, c * SPAN:(c + 1) * SPAN], gr[k, c])
-            near += nt(av[feat, c], gr[k, c])
-        wgrad[0:FC, lanes] = mine
-        wgrad[FC:2 * FC, lanes] = near
+        direct[:, c * SPAN:(c + 1) * SPAN] = dot(wself[...], gr[c].reshape(4 * FC, SPAN))
+    mine, near = jnp.zeros((FC, 4 * FC), F32), jnp.zeros((FC, 4 * FC), F32)
+    for c in range(PARTS):
+        grads = gr[c].reshape(4 * FC, SPAN)
+        mine += nt(xfull[feat, :, c * SPAN:(c + 1) * SPAN], grads)
+        near += nt(av[c, feat], grads)
+    wgrad[0:FC] = mine
+    wgrad[FC:2 * FC] = near
     for c in range(PARTS):
         for k in ORDER:
             shop(c, k, True).wait_recv()
@@ -561,7 +552,7 @@
         scratch_shapes=[
             pltpu.VMEM((PARTS, 3, TPN // PARTS, FC, TILE), jnp.int16), pltpu.VMEM((PARTS, 3, 8, TILE), F32),
             pltpu.VMEM((PARTS, 3, TPN // PARTS, FC, TILE), jnp.int16), pltpu.VMEM((PARTS, 3, 8, TILE), F32),
-            pltpu.VMEM((4, PARTS, FC, ROWS // PARTS), BF), pltpu.VMEM((4, PARTS, FC, ROWS // PARTS), BF),
+            pltpu.VMEM((PARTS, 4, FC, ROWS // PARTS), BF), pltpu.VMEM((PARTS, 4, FC, ROWS // PARTS), BF),
             dma((6 * PARTS,)), dma((6 * PARTS,)), dma((PARTS, 3, 2)), dma((PARTS, 3, 2)),
             dma((PARTS, 3)), dma((PARTS, 3)),
         ],

time: 97.2 us -> 97.3 us (level)
  Pallas kernels: 92.8 us -> 93.8 us
where the time goes in v7:
time: 97.3 us; the launch traced here: 96.5 us
  Pallas kernels  93.8 us (96%)
  local copies, waits for them, and re-layouts  1.38 us (1%)
  between operations  1.36 us (1%)
    pallas_call x1, Pallas kernels, scatter(): pl.pallas_call(scatter_kernel, out_shape=(jax.ShapeDtypeStruct((FC, ROWS)...  30.8 us
    pallas_call x1, Pallas kernels, gather(): pl.pallas_call(gather_kernel, out_shape=(OUT((NY, NZ, TPN, FC, TILE), BF)...  29.9 us
    pallas_call x1, Pallas kernels, dense(): pl.pallas_call(dense_kernel, out_shape=(jax.ShapeDtypeStruct((FC, ROWS),...  25.4 us
    pallas_call x1, Pallas kernels, backward(): pl.pallas_call(backward_kernel, out_shape=(OUT((NY, NZ, TPN, FC, TILE), B...  4.29 us
    pallas_call x1, Pallas kernels, forward(): pl.pallas_call(forward_kernel, out_shape=OUT((NX, TPN, FC + CNT, TILE), F...  3.43 us

profile of v7, /device:TPU:24, one launch (start us, length us, event | category | flops | bytes accessed | tf_op | source)
XLA Modules:
  0.0 96.5 jit_solution(14048490402365321125)
XLA Ops:
  1.3 29.9 %gather.1 = (bf16[2,8,8,64,128]{4,3,2,1,0:T(8,128)(2,1)S(1)}, bf16[4,64,1024]{2,1,0:T(8,128)(2,1)S(1)}, bf16[4,2,64,256]{3,2,1,0:T(8,128)(2,1)S(1)}, s16[4,256,16,128]{3,2,1,0:T(8,128)(2,1)S(1)}, s32[16,128]{1,0:T(8,128)S(1)}) custom-call(bf16[64,1024]{1,0:T(8,128)(2,1)} %bitcast.8, bf16[64,256]{1,0:T(8,128)(2,1)} %wself.3, bf16[64,256]{1,0:T(8,128)(2,1)} %wneigh.3, ...), custom_call_target="tpu_custom_call" | custom-call | tf_op jit(solution)/shard_map/gather/pallas_call | solution.py:343
  31.2 0.0 copy-start
  31.2 0.0 copy-start.1
  31.2 0.0 copy-start.2
  31.2 3.4 %forward_sums.1.part = f32[4,8,80,128]{3,2,1,0:T(8,128)S(1)} custom-call(s32[16,128]{1,0:T(8,128)S(1)} %get-tuple-element.17.slots, s16[4,256,16,128]{3,2,1,0:T(8,128)(2,1)S(1)} %get-tuple-element.18.edges, bf16[2,8,8,64,128]{4,3,2,1,0:T(8,128)(2,1)S(1)} %get-tuple-element.19.full), custom_call_target="tpu_custom_call" | custom-call | tf_op jit(solution)/shard_map/forward_sums/pallas_call | solution.py:404
  34.6 0.0 copy-done
  34.7 0.0 copy-done.1
  34.7 0.0 copy-done.2
  34.7 25.4 %dense.1 = (f32[64,1024]{1,0:T(8,128)S(1)}, f32[64,1024]{1,0:T(8,128)S(1)}, bf16[4,8,64,128]{3,2,1,0:T(8,128)(2,1)S(1)}, f32[128,256]{1,0:T(8,128)S(1)}) custom-call(f32[4,8,80,128]{3,2,1,0:T(8,128)S(1)} %forward_sums.1.part, bf16[4,64,1024]{2,1,0:T(8,128)(2,1)S(1)} %get-tuple-element.20.xfull, bf16[4,2,64,256]{3,2,1,0:T(8,128)(2,1)S(1)} %get-tuple-element.21.wfull, ...), custom_call_target="tpu_custom_call" | custom-call | tf_op jit(solution)/shard_map/dense/pallas_call | solution.py:542
  60.1 4.3 %backward_sums.1 = (bf16[2,8,8,64,128]{4,3,2,1,0:T(8,128)(2,1)S(1)}, f32[64,1024]{1,0:T(8,128)}) custom-call(s32[16,128]{1,0:T(8,128)S(1)} %get-tuple-element.17.slots, s16[4,256,16,128]{3,2,1,0:T(8,128)(2,1)S(1)} %get-tuple-element.18.edges, bf16[4,8,64,128]{3,2,1,0:T(8,128)(2,1)S(1)} %get-tuple-element.22.source, f32[64,1024]{1,0:T(8,128)S(1)} %get-tuple-element.23.act), custom_call_target="tpu_custom_call" | custom-call | tf_op jit(solution)/shard_map/backward_sums/pallas_call | solution.py:591
  64.3 30.8 %scatter.1 = (f32[64,1024]{1,0:T(8,128)S(1)}, f32[128,256]{1,0:T(8,128)S(1)}) custom-call(bf16[2,8,8,64,128]{4,3,2,1,0:T(8,128)(2,1)S(1)} %get-tuple-element.25.part, f32[128,256]{1,0:T(8,128)S(1)} %get-tuple-element.26.wgrad, f32[64,1024]{1,0:T(8,128)S(1)} %get-tuple-element.27.direct), custom_call_target="tpu_custom_call" | custom-call | tf_op jit(solution)/shard_map/scatter/pallas_call | solution.py:768
  95.1 0.7 fusion
  95.8 0.7 copy.14
Async XLA Ops:
  31.2 3.5 %copy-start = (f32[1024,64]{0,1:T(8,128)S(1)}, f32[1024,64]{0,1:T(8,128)}, u32[]{:S(2)}) copy-start(f32[1024,64]{0,1:T(8,128)} %param.15) | copy-start | bytes 786436
  31.2 3.5 %copy-start.1 = (bf16[64,256]{1,0:T(8,128)(2,1)S(1)}, bf16[64,256]{1,0:T(8,128)(2,1)}, u32[]{:S(2)}) copy-start(bf16[64,256]{1,0:T(8,128)(2,1)} %wself.3) | copy-start | bytes 98308
  31.2 3.5 %copy-start.2 = (bf16[64,256]{1,0:T(8,128)(2,1)S(1)}, bf16[64,256]{1,0:T(8,128)(2,1)}, u32[]{:S(2)}) copy-start(bf16[64,256]{1,0:T(8,128)(2,1)} %wneigh.3) | copy-start | bytes 98308
